TPU v7x, 256 devices: a whole 4x4x8 slice. The times are simulated.
256 devices in a mesh: seq: 32 (over z, x_lo, core), head: 8 (over x_hi, y).
Axes of the slice: x: 4 (x_hi: 2, x_lo: 2; x = x_hi * 2 + x_lo), y: 4, z: 8, core: 2. Of those that a mesh axis runs over, the one named last changes fastest.
Arguments:
- queries: bfloat16 [6144, 5120], P('seq', 'head'), may hold values from -8 to 8
- cur_keys: bfloat16 [6144, 5120], P('seq', 'head'), may hold values from -8 to 8
- cur_values: bfloat16 [6144, 5120], P('seq', 'head'), may hold values from -6 to 6
- hist_keys: bfloat16 [14336, 5120], P('seq', 'head'), may hold values from -8 to 8
- hist_values: bfloat16 [14336, 5120], P('seq', 'head'), may hold values from -6 to 6
- piece_readers: int32 [448, 2], P('seq'), may hold values from 0 to 31, as said below
- out_weight: bfloat16 [5120, 5120], P('head'), may hold values from -0.3125 to 0.3125
Outputs:
- attn_out: bfloat16 [6144, 5120], P('seq', 'head')
Inputs may be any that keep to these rules, and one draw needn't show every extreme that they name: `piece_readers`: row j names 2 different reader blocks (indices of seq); piece j is held by index j // 14 of seq. One holder sends at most 2 pieces to one reader block: each holder sends to exactly 14 reader blocks, 2 pieces to each, and in every draw one reader block receives 2 pieces from every holder.
All inputs are finite; a program needn't handle non-finite values.
Results may differ from a plain program's by a relative error of at most 0.018.
Values may be sent and summed in bfloat16 or wider, within the bound.
No kernel may reach another device: no remote copies, remote signals or barrier semaphores. Data moves between devices by JAX's collectives and lax.ppermute only.
A program may use at most 192 MiB of HBM per device.

v0:
```python
import math

import jax
import jax.numpy as jnp
from jax import lax
from jax.sharding import PartitionSpec as P

HDIM = 128
CAP = 2


def passed_along(value, axis, by):
    length = lax.axis_size(axis)
    return lax.ppermute(value, axis, [(i, (i + by) % length) for i in range(length)])


def attend(totals, query_heads, key_val, valid_keys):
    run_max, run_num, run_sum = totals
    head_count = query_heads.shape[1]
    key_heads = key_val[0].reshape(-1, head_count, HDIM)
    val_heads = key_val[1].reshape(-1, head_count, HDIM)
    scores = jnp.einsum("qhd,khd->hqk", query_heads, key_heads, preferred_element_type=jnp.float32)
    scores = scores * (1.0 / math.sqrt(HDIM))
    if valid_keys is not None:
        scores = jnp.where(valid_keys[None, None, :], scores, -1e30)
    new_max = jnp.maximum(run_max, jnp.max(scores, axis=-1))
    weights = jnp.exp(scores - new_max[..., None])
    if valid_keys is not None:
        weights = jnp.where(valid_keys[None, None, :], weights, 0.0)
    fade_by = jnp.exp(run_max - new_max)
    product = jnp.einsum(
        "hqk,khd->hqd", weights.astype(jnp.bfloat16), val_heads, preferred_element_type=jnp.float32
    )
    run_num = run_num * fade_by[..., None] + product
    run_sum = run_sum * fade_by + jnp.sum(weights, axis=-1)
    return (new_max, run_num, run_sum)


def local(queries, cur_keys, cur_values, hist_keys, hist_values, piece_readers, out_weight):
    tok_rows = queries.shape[0]
    width = queries.shape[1]
    head_count = width // HDIM
    query_heads = queries.reshape(tok_rows, head_count, HDIM)
    reader_count = lax.axis_size("seq")
    owner_rows = piece_readers.shape[0]
    piece_len = hist_keys.shape[0] // owner_rows
    reader_ids = jnp.arange(reader_count, dtype=jnp.int32)
    hits = jnp.sum(
        (piece_readers[:, :, None] == reader_ids[None, None, :]).astype(jnp.int32), axis=1
    )
    earlier = jnp.cumsum(hits, axis=0) - hits
    slot_ids = jnp.arange(CAP, dtype=jnp.int32)
    select = hits[None, :, :] * (earlier[None, :, :] == slot_ids[:, None, None]).astype(jnp.int32)
    select = jnp.transpose(select, (2, 0, 1))
    slot_full = jnp.sum(select, axis=2)[None, :, :]
    stacked = jnp.stack([hist_keys, hist_values]).reshape(2, owner_rows, piece_len * width)
    outgoing = jnp.einsum(
        "rcp,spx->srcx", select.astype(jnp.bfloat16), stacked, preferred_element_type=jnp.float32
    ).astype(jnp.bfloat16)
    arrived, arrived_full = (
        lax.all_to_all(outgoing, "seq", split_axis=1, concat_axis=1, tiled=True),
        lax.all_to_all(slot_full, "seq", split_axis=1, concat_axis=1, tiled=True),
    )
    hist_kv = arrived.reshape(2, -1, width)
    valid_keys = jnp.repeat(arrived_full.reshape(-1), piece_len) > 0
    start_totals = (
        jnp.full((head_count, tok_rows), -1e30, jnp.float32),
        jnp.zeros((head_count, tok_rows, HDIM), jnp.float32),
        jnp.zeros((head_count, tok_rows), jnp.float32),
    )
    totals = attend(start_totals, query_heads, hist_kv, valid_keys)
    own_block = jnp.stack([cur_keys, cur_values])
    totals = attend(totals, query_heads, own_block, None)

    def cycle_turn(step_idx, loop_state):
        travel, inner = loop_state
        travel = passed_along(travel, "seq", 1)
        return (travel, attend(inner, query_heads, travel, None))

    travel_end, totals = lax.fori_loop(0, reader_count - 1, cycle_turn, (own_block, totals))
    run_max, run_num, run_sum = totals
    attended = run_num / run_sum[..., None]
    attended = jnp.transpose(attended, (1, 0, 2)).reshape(tok_rows, width).astype(jnp.bfloat16)
    partial_out = jnp.dot(attended, out_weight, preferred_element_type=jnp.float32)
    return lax.psum_scatter(
        partial_out.astype(jnp.bfloat16), "head", scatter_dimension=1, tiled=True
    )


def solution(mesh):
    placed = (
        P("seq", "head"),
        P("seq", "head"),
        P("seq", "head"),
        P("seq", "head"),
        P("seq", "head"),
        P("seq", None),
        P("head", None),
    )
    return jax.shard_map(
        local, mesh=mesh, in_specs=placed, out_specs=P("seq", "head"), check_vma=False
    )
```

profile of v0, /device:TPU:32, one launch (start us, length us, event | category | flops | bytes accessed | tf_op | source)
XLA Modules:
  0.0 659.6 jit_solution(7990878650289596860)
XLA Ops:
  8.2 9.7 %all-to-all-start = ((s32[1,32,2]{2,0,1:T(1,128)}), s32[1,32,2]{2,0,1:T(1,128)S(1)}, u32[]{:S(2)}, u32[]{:S(2)}) async-start(s32[1,32,2]{2,0,1:T(1,128)} %copy.61), calls=%async_computation | async-start | bytes 32768 | tf_op jit(solution)/shard_map/all_to_all | solution.py:62
  17.8 1.5 stack.21
  20.8 3.9 fusion.4
  24.7 10.3 %copy.62 = bf16[2,32,2,20480]{3,2,0,1:T(2,128)(2,1)} copy(bf16[2,32,2,20480]{3,1,2,0:T(8,128)(2,1)} %fusion.4) | data formatting | bytes 10485760 | tf_op jit(solution)/shard_map/convert_element_type | solution.py:59
  35.0 8.5 %all-to-all-start.1 = ((bf16[2,32,2,20480]{3,2,0,1:T(2,128)(2,1)}), bf16[2,32,2,20480]{3,2,0,1:T(2,128)(2,1)}, u32[]{:S(2)}, u32[]{:S(2)}) async-start(bf16[2,32,2,20480]{3,2,0,1:T(2,128)(2,1)} %copy.62), calls=%async_computation.1 | async-start | bytes 10485760 | tf_op jit(solution)/shard_map/all_to_all | solution.py:61
  46.8 114.7 %all-to-all-done.1 = bf16[2,32,2,20480]{3,2,0,1:T(2,128)(2,1)} async-done(((bf16[2,32,2,20480]{3,2,0,1:T(2,128)(2,1)}), bf16[2,32,2,20480]{3,2,0,1:T(2,128)(2,1)}, u32[]{:S(2)}, u32[]{:S(2)}) %all-to-all-start.1) | async-done | bytes 5242912 | tf_op jit(solution)/shard_map/all_to_all | solution.py:61
  161.4 8.5 %fusion.47 = (bf16[1,32,2,20480]{3,2,0,1:T(2,128)(2,1)S(1)}, bf16[1,32,2,20480]{3,2,0,1:T(2,128)(2,1)}) fusion(bf16[2,32,2,20480]{3,2,0,1:T(2,128)(2,1)} %all-to-all-done.1), kind=kLoop, calls=%fused_computation.61 | loop fusion | bytes 10485760 | tf_op jit(solution)/shard_map/slice | solution.py:21
  169.9 8.0 %reshape_squeeze.6 = bf16[2048,5,128]{2,1,0:T(8,128)(2,1)} reshape(bf16[1,32,2,20480]{3,2,0,1:T(2,128)(2,1)} %get-tuple-element.79) | data formatting | bytes 5242880 | tf_op jit(solution)/shard_map/reshape;squeeze | solution.py:20
  178.0 3.6 reshape_squeeze.7
  181.5 3.8 bitcast_reduce_fusion
  185.4 2.0 fusion.7
  187.8 2.3 fusion.23
  190.5 350.5 %while.16 = (s32[]{:T(128)}, bf16[2,192,640]{2,1,0:T(8,128)(2,1)S(1)}, f32[5,192]{1,0:T(8,128)S(1)}, f32[5,192,128]{2,1,0:T(8,128)S(1)}, f32[5,192]{1,0:T(8,128)...) while((s32[]{:T(128)}, bf16[2,192,640]{2,1,0:T(8,128)(2,1)S(1)}, f32[5,192]{1,0:T(8,128)S(1)}, ...), condition=%wide.region_10.11_spmd, body=%wide.region_7.10_spmd.sunk | while | flops 95725440 | bytes 8908917 | solution.py:80
  190.6 9.1 %collective-permute-done = bf16[2,192,640]{2,1,0:T(8,128)(2,1)S(1)} collective-permute-done((bf16[2,192,640]{2,1,0:T(8,128)(2,1)S(1)}, bf16[2,192,640]{2,1,0:T(8,128)(2,1)S(1)}, u32[]{:S(2)}, u32[]{:S(2)}) %collective-permute-start) | collective-permute-done | bytes 491552 | tf_op jit(solution)/shard_map/while/body/eval_jaxpr/ppermute | solution.py:14
  201.4 9.1 %collective-permute-done = bf16[2,192,640]{2,1,0:T(8,128)(2,1)S(1)} collective-permute-done((bf16[2,192,640]{2,1,0:T(8,128)(2,1)S(1)}, bf16[2,192,640]{2,1,0:T(8,128)(2,1)S(1)}, u32[]{:S(2)}, u32[]{:S(2)}) %collective-permute-start) | collective-permute-done | bytes 491552 | tf_op jit(solution)/shard_map/while/body/eval_jaxpr/ppermute | solution.py:14
  212.2 9.1 %collective-permute-done = bf16[2,192,640]{2,1,0:T(8,128)(2,1)S(1)} collective-permute-done((bf16[2,192,640]{2,1,0:T(8,128)(2,1)S(1)}, bf16[2,192,640]{2,1,0:T(8,128)(2,1)S(1)}, u32[]{:S(2)}, u32[]{:S(2)}) %collective-permute-start) | collective-permute-done | bytes 491552 | tf_op jit(solution)/shard_map/while/body/eval_jaxpr/ppermute | solution.py:14
  223.1 9.1 %collective-permute-done = bf16[2,192,640]{2,1,0:T(8,128)(2,1)S(1)} collective-permute-done((bf16[2,192,640]{2,1,0:T(8,128)(2,1)S(1)}, bf16[2,192,640]{2,1,0:T(8,128)(2,1)S(1)}, u32[]{:S(2)}, u32[]{:S(2)}) %collective-permute-start) | collective-permute-done | bytes 491552 | tf_op jit(solution)/shard_map/while/body/eval_jaxpr/ppermute | solution.py:14
  233.9 9.1 %collective-permute-done = bf16[2,192,640]{2,1,0:T(8,128)(2,1)S(1)} collective-permute-done((bf16[2,192,640]{2,1,0:T(8,128)(2,1)S(1)}, bf16[2,192,640]{2,1,0:T(8,128)(2,1)S(1)}, u32[]{:S(2)}, u32[]{:S(2)}) %collective-permute-start) | collective-permute-done | bytes 491552 | tf_op jit(solution)/shard_map/while/body/eval_jaxpr/ppermute | solution.py:14
  244.7 9.1 %collective-permute-done = bf16[2,192,640]{2,1,0:T(8,128)(2,1)S(1)} collective-permute-done((bf16[2,192,640]{2,1,0:T(8,128)(2,1)S(1)}, bf16[2,192,640]{2,1,0:T(8,128)(2,1)S(1)}, u32[]{:S(2)}, u32[]{:S(2)}) %collective-permute-start) | collective-permute-done | bytes 491552 | tf_op jit(solution)/shard_map/while/body/eval_jaxpr/ppermute | solution.py:14
  255.5 9.1 %collective-permute-done = bf16[2,192,640]{2,1,0:T(8,128)(2,1)S(1)} collective-permute-done((bf16[2,192,640]{2,1,0:T(8,128)(2,1)S(1)}, bf16[2,192,640]{2,1,0:T(8,128)(2,1)S(1)}, u32[]{:S(2)}, u32[]{:S(2)}) %collective-permute-start) | collective-permute-done | bytes 491552 | tf_op jit(solution)/shard_map/while/body/eval_jaxpr/ppermute | solution.py:14
  266.3 9.1 %collective-permute-done = bf16[2,192,640]{2,1,0:T(8,128)(2,1)S(1)} collective-permute-done((bf16[2,192,640]{2,1,0:T(8,128)(2,1)S(1)}, bf16[2,192,640]{2,1,0:T(8,128)(2,1)S(1)}, u32[]{:S(2)}, u32[]{:S(2)}) %collective-permute-start) | collective-permute-done | bytes 491552 | tf_op jit(solution)/shard_map/while/body/eval_jaxpr/ppermute | solution.py:14
  277.1 9.1 %collective-permute-done = bf16[2,192,640]{2,1,0:T(8,128)(2,1)S(1)} collective-permute-done((bf16[2,192,640]{2,1,0:T(8,128)(2,1)S(1)}, bf16[2,192,640]{2,1,0:T(8,128)(2,1)S(1)}, u32[]{:S(2)}, u32[]{:S(2)}) %collective-permute-start) | collective-permute-done | bytes 491552 | tf_op jit(solution)/shard_map/while/body/eval_jaxpr/ppermute | solution.py:14
  287.9 9.1 %collective-permute-done = bf16[2,192,640]{2,1,0:T(8,128)(2,1)S(1)} collective-permute-done((bf16[2,192,640]{2,1,0:T(8,128)(2,1)S(1)}, bf16[2,192,640]{2,1,0:T(8,128)(2,1)S(1)}, u32[]{:S(2)}, u32[]{:S(2)}) %collective-permute-start) | collective-permute-done | bytes 491552 | tf_op jit(solution)/shard_map/while/body/eval_jaxpr/ppermute | solution.py:14
  298.7 9.1 %collective-permute-done = bf16[2,192,640]{2,1,0:T(8,128)(2,1)S(1)} collective-permute-done((bf16[2,192,640]{2,1,0:T(8,128)(2,1)S(1)}, bf16[2,192,640]{2,1,0:T(8,128)(2,1)S(1)}, u32[]{:S(2)}, u32[]{:S(2)}) %collective-permute-start) | collective-permute-done | bytes 491552 | tf_op jit(solution)/shard_map/while/body/eval_jaxpr/ppermute | solution.py:14
  309.6 9.1 %collective-permute-done = bf16[2,192,640]{2,1,0:T(8,128)(2,1)S(1)} collective-permute-done((bf16[2,192,640]{2,1,0:T(8,128)(2,1)S(1)}, bf16[2,192,640]{2,1,0:T(8,128)(2,1)S(1)}, u32[]{:S(2)}, u32[]{:S(2)}) %collective-permute-start) | collective-permute-done | bytes 491552 | tf_op jit(solution)/shard_map/while/body/eval_jaxpr/ppermute | solution.py:14
  320.4 9.1 %collective-permute-done = bf16[2,192,640]{2,1,0:T(8,128)(2,1)S(1)} collective-permute-done((bf16[2,192,640]{2,1,0:T(8,128)(2,1)S(1)}, bf16[2,192,640]{2,1,0:T(8,128)(2,1)S(1)}, u32[]{:S(2)}, u32[]{:S(2)}) %collective-permute-start) | collective-permute-done | bytes 491552 | tf_op jit(solution)/shard_map/while/body/eval_jaxpr/ppermute | solution.py:14
  331.2 9.1 %collective-permute-done = bf16[2,192,640]{2,1,0:T(8,128)(2,1)S(1)} collective-permute-done((bf16[2,192,640]{2,1,0:T(8,128)(2,1)S(1)}, bf16[2,192,640]{2,1,0:T(8,128)(2,1)S(1)}, u32[]{:S(2)}, u32[]{:S(2)}) %collective-permute-start) | collective-permute-done | bytes 491552 | tf_op jit(solution)/shard_map/while/body/eval_jaxpr/ppermute | solution.py:14
  342.0 9.1 %collective-permute-done = bf16[2,192,640]{2,1,0:T(8,128)(2,1)S(1)} collective-permute-done((bf16[2,192,640]{2,1,0:T(8,128)(2,1)S(1)}, bf16[2,192,640]{2,1,0:T(8,128)(2,1)S(1)}, u32[]{:S(2)}, u32[]{:S(2)}) %collective-permute-start) | collective-permute-done | bytes 491552 | tf_op jit(solution)/shard_map/while/body/eval_jaxpr/ppermute | solution.py:14
  352.8 9.1 %collective-permute-done = bf16[2,192,640]{2,1,0:T(8,128)(2,1)S(1)} collective-permute-done((bf16[2,192,640]{2,1,0:T(8,128)(2,1)S(1)}, bf16[2,192,640]{2,1,0:T(8,128)(2,1)S(1)}, u32[]{:S(2)}, u32[]{:S(2)}) %collective-permute-start) | collective-permute-done | bytes 491552 | tf_op jit(solution)/shard_map/while/body/eval_jaxpr/ppermute | solution.py:14
  363.6 9.1 %collective-permute-done = bf16[2,192,640]{2,1,0:T(8,128)(2,1)S(1)} collective-permute-done((bf16[2,192,640]{2,1,0:T(8,128)(2,1)S(1)}, bf16[2,192,640]{2,1,0:T(8,128)(2,1)S(1)}, u32[]{:S(2)}, u32[]{:S(2)}) %collective-permute-start) | collective-permute-done | bytes 491552 | tf_op jit(solution)/shard_map/while/body/eval_jaxpr/ppermute | solution.py:14
  374.4 9.1 %collective-permute-done = bf16[2,192,640]{2,1,0:T(8,128)(2,1)S(1)} collective-permute-done((bf16[2,192,640]{2,1,0:T(8,128)(2,1)S(1)}, bf16[2,192,640]{2,1,0:T(8,128)(2,1)S(1)}, u32[]{:S(2)}, u32[]{:S(2)}) %collective-permute-start) | collective-permute-done | bytes 491552 | tf_op jit(solution)/shard_map/while/body/eval_jaxpr/ppermute | solution.py:14
  385.2 9.7 %collective-permute-done = bf16[2,192,640]{2,1,0:T(8,128)(2,1)S(1)} collective-permute-done((bf16[2,192,640]{2,1,0:T(8,128)(2,1)S(1)}, bf16[2,192,640]{2,1,0:T(8,128)(2,1)S(1)}, u32[]{:S(2)}, u32[]{:S(2)}) %collective-permute-start) | collective-permute-done | bytes 491552 | tf_op jit(solution)/shard_map/while/body/eval_jaxpr/ppermute | solution.py:14
  396.6 10.4 %collective-permute-done = bf16[2,192,640]{2,1,0:T(8,128)(2,1)S(1)} collective-permute-done((bf16[2,192,640]{2,1,0:T(8,128)(2,1)S(1)}, bf16[2,192,640]{2,1,0:T(8,128)(2,1)S(1)}, u32[]{:S(2)}, u32[]{:S(2)}) %collective-permute-start) | collective-permute-done | bytes 491552 | tf_op jit(solution)/shard_map/while/body/eval_jaxpr/ppermute | solution.py:14
  408.6 10.4 %collective-permute-done = bf16[2,192,640]{2,1,0:T(8,128)(2,1)S(1)} collective-permute-done((bf16[2,192,640]{2,1,0:T(8,128)(2,1)S(1)}, bf16[2,192,640]{2,1,0:T(8,128)(2,1)S(1)}, u32[]{:S(2)}, u32[]{:S(2)}) %collective-permute-start) | collective-permute-done | bytes 491552 | tf_op jit(solution)/shard_map/while/body/eval_jaxpr/ppermute | solution.py:14
  420.7 10.4 %collective-permute-done = bf16[2,192,640]{2,1,0:T(8,128)(2,1)S(1)} collective-permute-done((bf16[2,192,640]{2,1,0:T(8,128)(2,1)S(1)}, bf16[2,192,640]{2,1,0:T(8,128)(2,1)S(1)}, u32[]{:S(2)}, u32[]{:S(2)}) %collective-permute-start) | collective-permute-done | bytes 491552 | tf_op jit(solution)/shard_map/while/body/eval_jaxpr/ppermute | solution.py:14
  432.7 10.4 %collective-permute-done = bf16[2,192,640]{2,1,0:T(8,128)(2,1)S(1)} collective-permute-done((bf16[2,192,640]{2,1,0:T(8,128)(2,1)S(1)}, bf16[2,192,640]{2,1,0:T(8,128)(2,1)S(1)}, u32[]{:S(2)}, u32[]{:S(2)}) %collective-permute-start) | collective-permute-done | bytes 491552 | tf_op jit(solution)/shard_map/while/body/eval_jaxpr/ppermute | solution.py:14
  444.7 10.4 %collective-permute-done = bf16[2,192,640]{2,1,0:T(8,128)(2,1)S(1)} collective-permute-done((bf16[2,192,640]{2,1,0:T(8,128)(2,1)S(1)}, bf16[2,192,640]{2,1,0:T(8,128)(2,1)S(1)}, u32[]{:S(2)}, u32[]{:S(2)}) %collective-permute-start) | collective-permute-done | bytes 491552 | tf_op jit(solution)/shard_map/while/body/eval_jaxpr/ppermute | solution.py:14
  456.7 10.4 %collective-permute-done = bf16[2,192,640]{2,1,0:T(8,128)(2,1)S(1)} collective-permute-done((bf16[2,192,640]{2,1,0:T(8,128)(2,1)S(1)}, bf16[2,192,640]{2,1,0:T(8,128)(2,1)S(1)}, u32[]{:S(2)}, u32[]{:S(2)}) %collective-permute-start) | collective-permute-done | bytes 491552 | tf_op jit(solution)/shard_map/while/body/eval_jaxpr/ppermute | solution.py:14
  468.8 10.4 %collective-permute-done = bf16[2,192,640]{2,1,0:T(8,128)(2,1)S(1)} collective-permute-done((bf16[2,192,640]{2,1,0:T(8,128)(2,1)S(1)}, bf16[2,192,640]{2,1,0:T(8,128)(2,1)S(1)}, u32[]{:S(2)}, u32[]{:S(2)}) %collective-permute-start) | collective-permute-done | bytes 491552 | tf_op jit(solution)/shard_map/while/body/eval_jaxpr/ppermute | solution.py:14
  480.8 10.4 %collective-permute-done = bf16[2,192,640]{2,1,0:T(8,128)(2,1)S(1)} collective-permute-done((bf16[2,192,640]{2,1,0:T(8,128)(2,1)S(1)}, bf16[2,192,640]{2,1,0:T(8,128)(2,1)S(1)}, u32[]{:S(2)}, u32[]{:S(2)}) %collective-permute-start) | collective-permute-done | bytes 491552 | tf_op jit(solution)/shard_map/while/body/eval_jaxpr/ppermute | solution.py:14
  492.8 10.4 %collective-permute-done = bf16[2,192,640]{2,1,0:T(8,128)(2,1)S(1)} collective-permute-done((bf16[2,192,640]{2,1,0:T(8,128)(2,1)S(1)}, bf16[2,192,640]{2,1,0:T(8,128)(2,1)S(1)}, u32[]{:S(2)}, u32[]{:S(2)}) %collective-permute-start) | collective-permute-done | bytes 491552 | tf_op jit(solution)/shard_map/while/body/eval_jaxpr/ppermute | solution.py:14
  504.8 10.4 %collective-permute-done = bf16[2,192,640]{2,1,0:T(8,128)(2,1)S(1)} collective-permute-done((bf16[2,192,640]{2,1,0:T(8,128)(2,1)S(1)}, bf16[2,192,640]{2,1,0:T(8,128)(2,1)S(1)}, u32[]{:S(2)}, u32[]{:S(2)}) %collective-permute-start) | collective-permute-done | bytes 491552 | tf_op jit(solution)/shard_map/while/body/eval_jaxpr/ppermute | solution.py:14
  516.9 10.4 %collective-permute-done = bf16[2,192,640]{2,1,0:T(8,128)(2,1)S(1)} collective-permute-done((bf16[2,192,640]{2,1,0:T(8,128)(2,1)S(1)}, bf16[2,192,640]{2,1,0:T(8,128)(2,1)S(1)}, u32[]{:S(2)}, u32[]{:S(2)}) %collective-permute-start) | collective-permute-done | bytes 491552 | tf_op jit(solution)/shard_map/while/body/eval_jaxpr/ppermute | solution.py:14
  528.9 10.4 %collective-permute-done = bf16[2,192,640]{2,1,0:T(8,128)(2,1)S(1)} collective-permute-done((bf16[2,192,640]{2,1,0:T(8,128)(2,1)S(1)}, bf16[2,192,640]{2,1,0:T(8,128)(2,1)S(1)}, u32[]{:S(2)}, u32[]{:S(2)}) %collective-permute-start) | collective-permute-done | bytes 491552 | tf_op jit(solution)/shard_map/while/body/eval_jaxpr/ppermute | solution.py:14
  541.4 4.6 convolution_convert_fusion.1
  546.0 2.6 copy.84
  548.6 102.3 %reduce-scatter.4.cloned.1.call-done = bf16[640,192]{1,0:T(8,128)(2,1)} async-done(((bf16[5120,192]{1,0:T(8,128)(2,1)}), bf16[640,192]{1,0:T(8,128)(2,1)}) %reduce-scatter.4.cloned.1.call-update) | async-done | bytes 245776
  650.9 1.8 copy.85
  (379 shorter events, 56.9 us)
Async XLA Ops:
  8.2 26.8 %all-to-all-start = ((s32[1,32,2]{2,0,1:T(1,128)}), s32[1,32,2]{2,0,1:T(1,128)S(1)}, u32[]{:S(2)}, u32[]{:S(2)}) async-start(s32[1,32,2]{2,0,1:T(1,128)} %copy.61), calls=%async_computation | async-start | bytes 32768 | tf_op jit(solution)/shard_map/all_to_all | solution.py:62
  35.0 8.5 %copy-start.5 = (bf16[192,640]{1,0:T(8,128)(2,1)S(1)}, bf16[192,640]{1,0:T(8,128)(2,1)}, u32[]{:S(2)}) copy-start(bf16[192,640]{1,0:T(8,128)(2,1)} %param.9) | copy-start | bytes 737284
  35.0 8.7 %copy-start.3 = (bf16[192,640]{1,0:T(8,128)(2,1)S(1)}, bf16[192,640]{1,0:T(8,128)(2,1)}, u32[]{:S(2)}) copy-start(bf16[192,640]{1,0:T(8,128)(2,1)} %param.10) | copy-start | bytes 737284
  35.0 8.9 %copy-start.2 = (bf16[192,640]{1,0:T(8,128)(2,1)S(1)}, bf16[192,640]{1,0:T(8,128)(2,1)}, u32[]{:S(2)}) copy-start(bf16[192,640]{1,0:T(8,128)(2,1)} %param.11) | copy-start | bytes 737284
  35.0 126.5 %all-to-all-start.1 = ((bf16[2,32,2,20480]{3,2,0,1:T(2,128)(2,1)}), bf16[2,32,2,20480]{3,2,0,1:T(2,128)(2,1)}, u32[]{:S(2)}, u32[]{:S(2)}) async-start(bf16[2,32,2,20480]{3,2,0,1:T(2,128)(2,1)} %copy.62), calls=%async_computation.1 | async-start | bytes 10485760 | tf_op jit(solution)/shard_map/all_to_all | solution.py:61
  43.5 607.5 %reduce-scatter.4.cloned.1.call-start = ((), (), s32[]{:S(2)}) async-start(), calls=%async_computation.3 | async-start | bytes 2949120
  185.3 2.0 copy-start
  185.3 2.5 copy-start.1
  187.8 2.7 copy-start.4
  190.5 9.2 %collective-permute-start = (bf16[2,192,640]{2,1,0:T(8,128)(2,1)S(1)}, bf16[2,192,640]{2,1,0:T(8,128)(2,1)S(1)}, u32[]{:S(2)}, u32[]{:S(2)}) collective-permute-start(bf16[2,192,640]{2,1,0:T(8,128)(2,1)S(1)} %get-tuple-element.144), channel_id=1, source_target_pairs={{0,8},{8,16},{16,24},{24,32},{32,40},{40,48},{48,56},{56,64},{64,7... | collective-permute-start | bytes 1474568 | tf_op jit(solution)/shard_map/while/body/eval_jaxpr/ppermute | solution.py:14
  201.3 9.2 %collective-permute-start = (bf16[2,192,640]{2,1,0:T(8,128)(2,1)S(1)}, bf16[2,192,640]{2,1,0:T(8,128)(2,1)S(1)}, u32[]{:S(2)}, u32[]{:S(2)}) collective-permute-start(bf16[2,192,640]{2,1,0:T(8,128)(2,1)S(1)} %get-tuple-element.144), channel_id=1, source_target_pairs={{0,8},{8,16},{16,24},{24,32},{32,40},{40,48},{48,56},{56,64},{64,7... | collective-permute-start | bytes 1474568 | tf_op jit(solution)/shard_map/while/body/eval_jaxpr/ppermute | solution.py:14
  212.2 9.2 %collective-permute-start = (bf16[2,192,640]{2,1,0:T(8,128)(2,1)S(1)}, bf16[2,192,640]{2,1,0:T(8,128)(2,1)S(1)}, u32[]{:S(2)}, u32[]{:S(2)}) collective-permute-start(bf16[2,192,640]{2,1,0:T(8,128)(2,1)S(1)} %get-tuple-element.144), channel_id=1, source_target_pairs={{0,8},{8,16},{16,24},{24,32},{32,40},{40,48},{48,56},{56,64},{64,7... | collective-permute-start | bytes 1474568 | tf_op jit(solution)/shard_map/while/body/eval_jaxpr/ppermute | solution.py:14
  223.0 9.2 %collective-permute-start = (bf16[2,192,640]{2,1,0:T(8,128)(2,1)S(1)}, bf16[2,192,640]{2,1,0:T(8,128)(2,1)S(1)}, u32[]{:S(2)}, u32[]{:S(2)}) collective-permute-start(bf16[2,192,640]{2,1,0:T(8,128)(2,1)S(1)} %get-tuple-element.144), channel_id=1, source_target_pairs={{0,8},{8,16},{16,24},{24,32},{32,40},{40,48},{48,56},{56,64},{64,7... | collective-permute-start | bytes 1474568 | tf_op jit(solution)/shard_map/while/body/eval_jaxpr/ppermute | solution.py:14
  233.8 9.2 %collective-permute-start = (bf16[2,192,640]{2,1,0:T(8,128)(2,1)S(1)}, bf16[2,192,640]{2,1,0:T(8,128)(2,1)S(1)}, u32[]{:S(2)}, u32[]{:S(2)}) collective-permute-start(bf16[2,192,640]{2,1,0:T(8,128)(2,1)S(1)} %get-tuple-element.144), channel_id=1, source_target_pairs={{0,8},{8,16},{16,24},{24,32},{32,40},{40,48},{48,56},{56,64},{64,7... | collective-permute-start | bytes 1474568 | tf_op jit(solution)/shard_map/while/body/eval_jaxpr/ppermute | solution.py:14
  244.6 9.2 %collective-permute-start = (bf16[2,192,640]{2,1,0:T(8,128)(2,1)S(1)}, bf16[2,192,640]{2,1,0:T(8,128)(2,1)S(1)}, u32[]{:S(2)}, u32[]{:S(2)}) collective-permute-start(bf16[2,192,640]{2,1,0:T(8,128)(2,1)S(1)} %get-tuple-element.144), channel_id=1, source_target_pairs={{0,8},{8,16},{16,24},{24,32},{32,40},{40,48},{48,56},{56,64},{64,7... | collective-permute-start | bytes 1474568 | tf_op jit(solution)/shard_map/while/body/eval_jaxpr/ppermute | solution.py:14
  255.4 9.2 %collective-permute-start = (bf16[2,192,640]{2,1,0:T(8,128)(2,1)S(1)}, bf16[2,192,640]{2,1,0:T(8,128)(2,1)S(1)}, u32[]{:S(2)}, u32[]{:S(2)}) collective-permute-start(bf16[2,192,640]{2,1,0:T(8,128)(2,1)S(1)} %get-tuple-element.144), channel_id=1, source_target_pairs={{0,8},{8,16},{16,24},{24,32},{32,40},{40,48},{48,56},{56,64},{64,7... | collective-permute-start | bytes 1474568 | tf_op jit(solution)/shard_map/while/body/eval_jaxpr/ppermute | solution.py:14
  266.2 9.2 %collective-permute-start = (bf16[2,192,640]{2,1,0:T(8,128)(2,1)S(1)}, bf16[2,192,640]{2,1,0:T(8,128)(2,1)S(1)}, u32[]{:S(2)}, u32[]{:S(2)}) collective-permute-start(bf16[2,192,640]{2,1,0:T(8,128)(2,1)S(1)} %get-tuple-element.144), channel_id=1, source_target_pairs={{0,8},{8,16},{16,24},{24,32},{32,40},{40,48},{48,56},{56,64},{64,7... | collective-permute-start | bytes 1474568 | tf_op jit(solution)/shard_map/while/body/eval_jaxpr/ppermute | solution.py:14
  277.0 9.2 %collective-permute-start = (bf16[2,192,640]{2,1,0:T(8,128)(2,1)S(1)}, bf16[2,192,640]{2,1,0:T(8,128)(2,1)S(1)}, u32[]{:S(2)}, u32[]{:S(2)}) collective-permute-start(bf16[2,192,640]{2,1,0:T(8,128)(2,1)S(1)} %get-tuple-element.144), channel_id=1, source_target_pairs={{0,8},{8,16},{16,24},{24,32},{32,40},{40,48},{48,56},{56,64},{64,7... | collective-permute-start | bytes 1474568 | tf_op jit(solution)/shard_map/while/body/eval_jaxpr/ppermute | solution.py:14
  287.8 9.2 %collective-permute-start = (bf16[2,192,640]{2,1,0:T(8,128)(2,1)S(1)}, bf16[2,192,640]{2,1,0:T(8,128)(2,1)S(1)}, u32[]{:S(2)}, u32[]{:S(2)}) collective-permute-start(bf16[2,192,640]{2,1,0:T(8,128)(2,1)S(1)} %get-tuple-element.144), channel_id=1, source_target_pairs={{0,8},{8,16},{16,24},{24,32},{32,40},{40,48},{48,56},{56,64},{64,7... | collective-permute-start | bytes 1474568 | tf_op jit(solution)/shard_map/while/body/eval_jaxpr/ppermute | solution.py:14
  298.7 9.2 %collective-permute-start = (bf16[2,192,640]{2,1,0:T(8,128)(2,1)S(1)}, bf16[2,192,640]{2,1,0:T(8,128)(2,1)S(1)}, u32[]{:S(2)}, u32[]{:S(2)}) collective-permute-start(bf16[2,192,640]{2,1,0:T(8,128)(2,1)S(1)} %get-tuple-element.144), channel_id=1, source_target_pairs={{0,8},{8,16},{16,24},{24,32},{32,40},{40,48},{48,56},{56,64},{64,7... | collective-permute-start | bytes 1474568 | tf_op jit(solution)/shard_map/while/body/eval_jaxpr/ppermute | solution.py:14
  309.5 9.2 %collective-permute-start = (bf16[2,192,640]{2,1,0:T(8,128)(2,1)S(1)}, bf16[2,192,640]{2,1,0:T(8,128)(2,1)S(1)}, u32[]{:S(2)}, u32[]{:S(2)}) collective-permute-start(bf16[2,192,640]{2,1,0:T(8,128)(2,1)S(1)} %get-tuple-element.144), channel_id=1, source_target_pairs={{0,8},{8,16},{16,24},{24,32},{32,40},{40,48},{48,56},{56,64},{64,7... | collective-permute-start | bytes 1474568 | tf_op jit(solution)/shard_map/while/body/eval_jaxpr/ppermute | solution.py:14
  320.3 9.2 %collective-permute-start = (bf16[2,192,640]{2,1,0:T(8,128)(2,1)S(1)}, bf16[2,192,640]{2,1,0:T(8,128)(2,1)S(1)}, u32[]{:S(2)}, u32[]{:S(2)}) collective-permute-start(bf16[2,192,640]{2,1,0:T(8,128)(2,1)S(1)} %get-tuple-element.144), channel_id=1, source_target_pairs={{0,8},{8,16},{16,24},{24,32},{32,40},{40,48},{48,56},{56,64},{64,7... | collective-permute-start | bytes 1474568 | tf_op jit(solution)/shard_map/while/body/eval_jaxpr/ppermute | solution.py:14
  331.1 9.2 %collective-permute-start = (bf16[2,192,640]{2,1,0:T(8,128)(2,1)S(1)}, bf16[2,192,640]{2,1,0:T(8,128)(2,1)S(1)}, u32[]{:S(2)}, u32[]{:S(2)}) collective-permute-start(bf16[2,192,640]{2,1,0:T(8,128)(2,1)S(1)} %get-tuple-element.144), channel_id=1, source_target_pairs={{0,8},{8,16},{16,24},{24,32},{32,40},{40,48},{48,56},{56,64},{64,7... | collective-permute-start | bytes 1474568 | tf_op jit(solution)/shard_map/while/body/eval_jaxpr/ppermute | solution.py:14
  341.9 9.2 %collective-permute-start = (bf16[2,192,640]{2,1,0:T(8,128)(2,1)S(1)}, bf16[2,192,640]{2,1,0:T(8,128)(2,1)S(1)}, u32[]{:S(2)}, u32[]{:S(2)}) collective-permute-start(bf16[2,192,640]{2,1,0:T(8,128)(2,1)S(1)} %get-tuple-element.144), channel_id=1, source_target_pairs={{0,8},{8,16},{16,24},{24,32},{32,40},{40,48},{48,56},{56,64},{64,7... | collective-permute-start | bytes 1474568 | tf_op jit(solution)/shard_map/while/body/eval_jaxpr/ppermute | solution.py:14
  352.7 9.2 %collective-permute-start = (bf16[2,192,640]{2,1,0:T(8,128)(2,1)S(1)}, bf16[2,192,640]{2,1,0:T(8,128)(2,1)S(1)}, u32[]{:S(2)}, u32[]{:S(2)}) collective-permute-start(bf16[2,192,640]{2,1,0:T(8,128)(2,1)S(1)} %get-tuple-element.144), channel_id=1, source_target_pairs={{0,8},{8,16},{16,24},{24,32},{32,40},{40,48},{48,56},{56,64},{64,7... | collective-permute-start | bytes 1474568 | tf_op jit(solution)/shard_map/while/body/eval_jaxpr/ppermute | solution.py:14
  363.5 9.2 %collective-permute-start = (bf16[2,192,640]{2,1,0:T(8,128)(2,1)S(1)}, bf16[2,192,640]{2,1,0:T(8,128)(2,1)S(1)}, u32[]{:S(2)}, u32[]{:S(2)}) collective-permute-start(bf16[2,192,640]{2,1,0:T(8,128)(2,1)S(1)} %get-tuple-element.144), channel_id=1, source_target_pairs={{0,8},{8,16},{16,24},{24,32},{32,40},{40,48},{48,56},{56,64},{64,7... | collective-permute-start | bytes 1474568 | tf_op jit(solution)/shard_map/while/body/eval_jaxpr/ppermute | solution.py:14
  374.3 9.2 %collective-permute-start = (bf16[2,192,640]{2,1,0:T(8,128)(2,1)S(1)}, bf16[2,192,640]{2,1,0:T(8,128)(2,1)S(1)}, u32[]{:S(2)}, u32[]{:S(2)}) collective-permute-start(bf16[2,192,640]{2,1,0:T(8,128)(2,1)S(1)} %get-tuple-element.144), channel_id=1, source_target_pairs={{0,8},{8,16},{16,24},{24,32},{32,40},{40,48},{48,56},{56,64},{64,7... | collective-permute-start | bytes 1474568 | tf_op jit(solution)/shard_map/while/body/eval_jaxpr/ppermute | solution.py:14
  385.2 9.8 %collective-permute-start = (bf16[2,192,640]{2,1,0:T(8,128)(2,1)S(1)}, bf16[2,192,640]{2,1,0:T(8,128)(2,1)S(1)}, u32[]{:S(2)}, u32[]{:S(2)}) collective-permute-start(bf16[2,192,640]{2,1,0:T(8,128)(2,1)S(1)} %get-tuple-element.144), channel_id=1, source_target_pairs={{0,8},{8,16},{16,24},{24,32},{32,40},{40,48},{48,56},{56,64},{64,7... | collective-permute-start | bytes 1474568 | tf_op jit(solution)/shard_map/while/body/eval_jaxpr/ppermute | solution.py:14
  396.5 10.4 %collective-permute-start = (bf16[2,192,640]{2,1,0:T(8,128)(2,1)S(1)}, bf16[2,192,640]{2,1,0:T(8,128)(2,1)S(1)}, u32[]{:S(2)}, u32[]{:S(2)}) collective-permute-start(bf16[2,192,640]{2,1,0:T(8,128)(2,1)S(1)} %get-tuple-element.144), channel_id=1, source_target_pairs={{0,8},{8,16},{16,24},{24,32},{32,40},{40,48},{48,56},{56,64},{64,7... | collective-permute-start | bytes 1474568 | tf_op jit(solution)/shard_map/while/body/eval_jaxpr/ppermute | solution.py:14
  408.5 10.4 %collective-permute-start = (bf16[2,192,640]{2,1,0:T(8,128)(2,1)S(1)}, bf16[2,192,640]{2,1,0:T(8,128)(2,1)S(1)}, u32[]{:S(2)}, u32[]{:S(2)}) collective-permute-start(bf16[2,192,640]{2,1,0:T(8,128)(2,1)S(1)} %get-tuple-element.144), channel_id=1, source_target_pairs={{0,8},{8,16},{16,24},{24,32},{32,40},{40,48},{48,56},{56,64},{64,7... | collective-permute-start | bytes 1474568 | tf_op jit(solution)/shard_map/while/body/eval_jaxpr/ppermute | solution.py:14
  420.6 10.4 %collective-permute-start = (bf16[2,192,640]{2,1,0:T(8,128)(2,1)S(1)}, bf16[2,192,640]{2,1,0:T(8,128)(2,1)S(1)}, u32[]{:S(2)}, u32[]{:S(2)}) collective-permute-start(bf16[2,192,640]{2,1,0:T(8,128)(2,1)S(1)} %get-tuple-element.144), channel_id=1, source_target_pairs={{0,8},{8,16},{16,24},{24,32},{32,40},{40,48},{48,56},{56,64},{64,7... | collective-permute-start | bytes 1474568 | tf_op jit(solution)/shard_map/while/body/eval_jaxpr/ppermute | solution.py:14
  432.6 10.4 %collective-permute-start = (bf16[2,192,640]{2,1,0:T(8,128)(2,1)S(1)}, bf16[2,192,640]{2,1,0:T(8,128)(2,1)S(1)}, u32[]{:S(2)}, u32[]{:S(2)}) collective-permute-start(bf16[2,192,640]{2,1,0:T(8,128)(2,1)S(1)} %get-tuple-element.144), channel_id=1, source_target_pairs={{0,8},{8,16},{16,24},{24,32},{32,40},{40,48},{48,56},{56,64},{64,7... | collective-permute-start | bytes 1474568 | tf_op jit(solution)/shard_map/while/body/eval_jaxpr/ppermute | solution.py:14
  444.6 10.4 %collective-permute-start = (bf16[2,192,640]{2,1,0:T(8,128)(2,1)S(1)}, bf16[2,192,640]{2,1,0:T(8,128)(2,1)S(1)}, u32[]{:S(2)}, u32[]{:S(2)}) collective-permute-start(bf16[2,192,640]{2,1,0:T(8,128)(2,1)S(1)} %get-tuple-element.144), channel_id=1, source_target_pairs={{0,8},{8,16},{16,24},{24,32},{32,40},{40,48},{48,56},{56,64},{64,7... | collective-permute-start | bytes 1474568 | tf_op jit(solution)/shard_map/while/body/eval_jaxpr/ppermute | solution.py:14
  456.6 10.4 %collective-permute-start = (bf16[2,192,640]{2,1,0:T(8,128)(2,1)S(1)}, bf16[2,192,640]{2,1,0:T(8,128)(2,1)S(1)}, u32[]{:S(2)}, u32[]{:S(2)}) collective-permute-start(bf16[2,192,640]{2,1,0:T(8,128)(2,1)S(1)} %get-tuple-element.144), channel_id=1, source_target_pairs={{0,8},{8,16},{16,24},{24,32},{32,40},{40,48},{48,56},{56,64},{64,7... | collective-permute-start | bytes 1474568 | tf_op jit(solution)/shard_map/while/body/eval_jaxpr/ppermute | solution.py:14
  468.7 10.4 %collective-permute-start = (bf16[2,192,640]{2,1,0:T(8,128)(2,1)S(1)}, bf16[2,192,640]{2,1,0:T(8,128)(2,1)S(1)}, u32[]{:S(2)}, u32[]{:S(2)}) collective-permute-start(bf16[2,192,640]{2,1,0:T(8,128)(2,1)S(1)} %get-tuple-element.144), channel_id=1, source_target_pairs={{0,8},{8,16},{16,24},{24,32},{32,40},{40,48},{48,56},{56,64},{64,7... | collective-permute-start | bytes 1474568 | tf_op jit(solution)/shard_map/while/body/eval_jaxpr/ppermute | solution.py:14
  480.7 10.4 %collective-permute-start = (bf16[2,192,640]{2,1,0:T(8,128)(2,1)S(1)}, bf16[2,192,640]{2,1,0:T(8,128)(2,1)S(1)}, u32[]{:S(2)}, u32[]{:S(2)}) collective-permute-start(bf16[2,192,640]{2,1,0:T(8,128)(2,1)S(1)} %get-tuple-element.144), channel_id=1, source_target_pairs={{0,8},{8,16},{16,24},{24,32},{32,40},{40,48},{48,56},{56,64},{64,7... | collective-permute-start | bytes 1474568 | tf_op jit(solution)/shard_map/while/body/eval_jaxpr/ppermute | solution.py:14
  492.7 10.4 %collective-permute-start = (bf16[2,192,640]{2,1,0:T(8,128)(2,1)S(1)}, bf16[2,192,640]{2,1,0:T(8,128)(2,1)S(1)}, u32[]{:S(2)}, u32[]{:S(2)}) collective-permute-start(bf16[2,192,640]{2,1,0:T(8,128)(2,1)S(1)} %get-tuple-element.144), channel_id=1, source_target_pairs={{0,8},{8,16},{16,24},{24,32},{32,40},{40,48},{48,56},{56,64},{64,7... | collective-permute-start | bytes 1474568 | tf_op jit(solution)/shard_map/while/body/eval_jaxpr/ppermute | solution.py:14
  504.7 10.4 %collective-permute-start = (bf16[2,192,640]{2,1,0:T(8,128)(2,1)S(1)}, bf16[2,192,640]{2,1,0:T(8,128)(2,1)S(1)}, u32[]{:S(2)}, u32[]{:S(2)}) collective-permute-start(bf16[2,192,640]{2,1,0:T(8,128)(2,1)S(1)} %get-tuple-element.144), channel_id=1, source_target_pairs={{0,8},{8,16},{16,24},{24,32},{32,40},{40,48},{48,56},{56,64},{64,7... | collective-permute-start | bytes 1474568 | tf_op jit(solution)/shard_map/while/body/eval_jaxpr/ppermute | solution.py:14
  516.8 10.4 %collective-permute-start = (bf16[2,192,640]{2,1,0:T(8,128)(2,1)S(1)}, bf16[2,192,640]{2,1,0:T(8,128)(2,1)S(1)}, u32[]{:S(2)}, u32[]{:S(2)}) collective-permute-start(bf16[2,192,640]{2,1,0:T(8,128)(2,1)S(1)} %get-tuple-element.144), channel_id=1, source_target_pairs={{0,8},{8,16},{16,24},{24,32},{32,40},{40,48},{48,56},{56,64},{64,7... | collective-permute-start | bytes 1474568 | tf_op jit(solution)/shard_map/while/body/eval_jaxpr/ppermute | solution.py:14
  528.8 10.4 %collective-permute-start = (bf16[2,192,640]{2,1,0:T(8,128)(2,1)S(1)}, bf16[2,192,640]{2,1,0:T(8,128)(2,1)S(1)}, u32[]{:S(2)}, u32[]{:S(2)}) collective-permute-start(bf16[2,192,640]{2,1,0:T(8,128)(2,1)S(1)} %get-tuple-element.144), channel_id=1, source_target_pairs={{0,8},{8,16},{16,24},{24,32},{32,40},{40,48},{48,56},{56,64},{64,7... | collective-permute-start | bytes 1474568 | tf_op jit(solution)/shard_map/while/body/eval_jaxpr/ppermute | solution.py:14
Sparse Core Ops, SparseCore 0:
  548.7 102.1 reduce-scatter.3
where the time goes:
time: 660 us
  waiting for transfers between devices  515 us (78%)
  local copies, waits for them, and re-layouts  54.7 us (8%)
  matrix products  43.6 us (7%)
  starting transfers between devices  20.7 us (3%)
  between operations  13.6 us (2%)
  other arithmetic  8.76 us (1%)
    ppermute x31, waiting for transfers between devices, passed_along(): lax.ppermute(value, axis, [(i, (i + by) % length) for i in range(length)])  298 us
    all_to_all x1, waiting for transfers between devices, local(): lax.all_to_all(outgoing, 'seq', split_axis=1, concat_axis=1, tiled=True)  115 us
    unnamed x2, waiting for transfers between devices  102 us
    dot_general x33, matrix products, attend(): jnp.einsum('hqk,khd->hqd', weights.astype(jnp.bfloat16), val_heads, prefe...  18.8 us
    dot_general x33, matrix products, attend(): jnp.einsum('qhd,khd->hqk', query_heads, key_heads, preferred_element_type...  16.3 us
    slice x63, local copies, waits for them, and re-layouts, attend(): val_heads = key_val[1].reshape(-1, head_count, HDIM)  15.4 us
  transfers between devices with their start and end apart: 34, of which 33 were waited for; matrix products, arithmetic and copies ran while one was open for 3% of the time, Pallas kernels for 0%

commit v1 on v0

v1 whole, which is shorter than its diff:
```python
import functools
import math

import jax
import jax.numpy as jnp
from jax import lax
from jax.experimental import pallas as pl
from jax.experimental.pallas import tpu as pltpu
from jax.sharding import PartitionSpec as P

HDIM = 128
PLANES = 8
GROUP = 4
ROWS = 192
HIST = 448
PIECE = 32
HELD = 14
YS = 4
COEF = math.log2(math.e) / math.sqrt(HDIM)
NEG = -1e30
CHUNKS = ((0, 5),)
OFFS = (4, 3, -3, 2, -2, 1, -1, 0)
BF = jnp.bfloat16
F32 = jnp.float32
ROUTE_V = ROWS
HIST_K = 2 * ROWS
HIST_V = 2 * ROWS + HIST


def seq_move(value, to):
    perm = []
    for z in range(PLANES):
        for x in range(2):
            for c in range(2):
                nz, nx, nc = to(z, x, c)
                perm.append((z * 4 + x * 2 + c, (nz % PLANES) * 4 + nx * 2 + nc))
    return lax.ppermute(value, "seq", perm)


def swap_core(value):
    return seq_move(value, lambda z, x, c: (z, x, 1 - c))


def swap_x(value):
    return seq_move(value, lambda z, x, c: (z, 1 - x, c))


def up(value):
    return seq_move(value, lambda z, x, c: (z + 1, x, c))


def down(value):
    return seq_move(value, lambda z, x, c: (z - 1, x, c))


def away(value):
    return seq_move(value, lambda z, x, c: (z + 1 - 2 * c, x, c))


def head_move(value, by_x, by_y):
    perm = []
    for x in range(2):
        for y in range(YS):
            perm.append((x * YS + y, ((x + by_x) % 2) * YS + (y + by_y) % YS))
    return lax.ppermute(value, "head", perm)


def attend_kernel(heads, first, *refs):
    table, bias = refs[0], refs[1]
    queries = refs[2:10]
    sources = refs[10:12]
    pos = 12
    if not first:
        prev_out, prev_stat = refs[pos : pos + 8], refs[pos + 8 : pos + 16]
        pos += 16
    outs, stats = refs[pos : pos + 8], refs[pos + 8 : pos + 16]
    scratch = refs[pos + 16]
    lane = lax.broadcasted_iota(jnp.int32, (ROWS, HDIM), 1)
    scratch[...] = jnp.zeros(scratch.shape, F32)

    def one_head(h, carry):
        cols = pl.ds(pl.multiple_of(h * HDIM, HDIM), HDIM)
        keys = jnp.concatenate([s[0:ROWS, cols] for s in sources], axis=0)
        vals = jnp.concatenate([s[ROWS : 2 * ROWS, cols] for s in sources], axis=0)
        for j in range(8):
            picks = [table[j, t] for t in range(4)]
            hist_k = [
                sources[t // 2][pl.ds(pl.multiple_of(HIST_K + picks[t] * PIECE, PIECE), PIECE), cols]
                for t in range(4)
            ]
            hist_v = [
                sources[t // 2][pl.ds(pl.multiple_of(HIST_V + picks[t] * PIECE, PIECE), PIECE), cols]
                for t in range(4)
            ]
            all_k = jnp.concatenate([keys] + hist_k, axis=0)
            all_v = jnp.concatenate([vals] + hist_v, axis=0)
            score = lax.dot_general(
                queries[j][:, cols], all_k, (((1,), (1,)), ((), ())), preferred_element_type=F32
            )
            score = jnp.concatenate(
                [score[:, : 2 * ROWS], score[:, 2 * ROWS :] + bias[j : j + 1, :]], axis=1
            )
            top = jnp.max(score, axis=1, keepdims=True) * COEF
            if not first:
                before = prev_stat[j][...]
                before = jnp.sum(jnp.where(lane == h, before, 0.0), axis=1, keepdims=True)
                top = jnp.maximum(top, before)
            weight = jnp.exp2(score * COEF - top)
            total = jnp.sum(weight, axis=1, keepdims=True)
            num = jnp.dot(weight.astype(BF), all_v, preferred_element_type=F32)
            if not first:
                keep = jnp.exp2(before - top)
                total = total + keep
                num = num + prev_out[j][:, cols] * keep
            num = num / total
            outs[j][:, cols] = num.astype(outs[j].dtype)
            level = top + jnp.log2(total)
            scratch[j, 0:ROWS, :] = jnp.where(lane == h, level, scratch[j, 0:ROWS, :])
        return carry

    lax.fori_loop(0, heads, one_head, 0)
    for j in range(8):
        if first:
            stats[j][...] = scratch[j, 0:ROWS, :]
        else:
            stats[j][...] = jnp.transpose(scratch[j])[0:8, :]


def attend(heads, table, bias, queries, sources, before):
    first = before is None
    width = heads * HDIM
    vmem = pl.BlockSpec(memory_space=pltpu.VMEM)
    smem = pl.BlockSpec(memory_space=pltpu.SMEM)
    args = [table, bias, *queries, *sources]
    if not first:
        args += [*before[0], *before[1]]
    out_type = F32 if first else BF
    stat_shape = (ROWS, HDIM) if first else (8, 256)
    shapes = [jax.ShapeDtypeStruct((ROWS, width), out_type)] * 8
    shapes += [jax.ShapeDtypeStruct(stat_shape, F32)] * 8
    keys = 2 * ROWS + 4 * PIECE
    result = pl.pallas_call(
        functools.partial(attend_kernel, heads, first),
        out_shape=shapes,
        in_specs=[smem] + [vmem] * (len(args) - 1),
        out_specs=[vmem] * 16,
        scratch_shapes=[pltpu.VMEM((8, 256, HDIM), F32)],
        compiler_params=pltpu.CompilerParams(vmem_limit_bytes=48 * 1024 * 1024),
        cost_estimate=pl.CostEstimate(
            flops=8 * heads * ROWS * keys * HDIM * 4,
            bytes_accessed=8 * ROWS * width * 6,
            transcendentals=8 * heads * ROWS * keys,
        ),
    )(*args)
    return result[:8], result[8:]


def blend(levels):
    top = functools.reduce(jnp.maximum, levels)
    parts = [jnp.exp2(v - top) for v in levels]
    total = functools.reduce(jnp.add, parts)
    shares = [p / total for p in parts]
    pad = jnp.zeros((HDIM - 8 * len(shares), 256), F32)
    columns = jnp.transpose(jnp.concatenate(shares + [pad], axis=0))
    return columns, top + jnp.log2(total)


def write_blend(heads, values, levels, out, stat):
    columns, level = blend(levels)
    for h in range(heads):
        cols = slice(h * HDIM, (h + 1) * HDIM)
        acc = None
        for i, v in enumerate(values):
            part = v[:, cols].astype(F32) * columns[0:ROWS, 8 * i + h : 8 * i + h + 1]
            acc = part if acc is None else acc + part
        out[:, cols] = acc.astype(BF)
    if stat is not None:
        stat[...] = level


def first_merge_kernel(heads, core, far_o, far_s, up_o, up_s, dn_o, dn_s, ou, su, od, sd):
    on_up = core[0] == 0
    far = far_s[...]
    low = jnp.full(far.shape, NEG, F32)
    write_blend(heads, [far_o, up_o], [jnp.where(on_up, far, low), up_s[...]], ou, su)
    write_blend(heads, [far_o, dn_o], [jnp.where(on_up, low, far), dn_s[...]], od, sd)


def merge_kernel(heads, ru_o, ru_s, rd_o, rd_s, up_o, up_s, dn_o, dn_s, ou, su, od, sd):
    write_blend(heads, [ru_o, up_o], [ru_s[...], up_s[...]], ou, su)
    write_blend(heads, [rd_o, dn_o], [rd_s[...], dn_s[...]], od, sd)


def last_merge_kernel(heads, ru_o, ru_s, rd_o, rd_s, own_o, own_s, out):
    write_blend(heads, [ru_o, rd_o, own_o], [ru_s[...], rd_s[...], own_s[...]], out, None)


def small_call(kernel, heads, args, pairs, scalar=False):
    width = heads * HDIM
    vmem = pl.BlockSpec(memory_space=pltpu.VMEM)
    smem = pl.BlockSpec(memory_space=pltpu.SMEM)
    value = jax.ShapeDtypeStruct((ROWS, width), BF)
    stat = jax.ShapeDtypeStruct((8, 256), F32)
    shapes = [value, stat] * pairs if pairs else value
    specs = [vmem] * len(args)
    if scalar:
        specs[0] = smem
    return pl.pallas_call(
        functools.partial(kernel, heads),
        out_shape=shapes,
        in_specs=specs,
        out_specs=[vmem] * (2 * pairs) if pairs else vmem,
        compiler_params=pltpu.CompilerParams(vmem_limit_bytes=32 * 1024 * 1024),
        cost_estimate=pl.CostEstimate(
            flops=6 * ROWS * width, bytes_accessed=12 * ROWS * width, transcendentals=8192
        ),
    )(*args)


def gather_queries(own):
    up1, dn1 = up(own), down(own)
    up2, dn2 = up(up1), down(dn1)
    up3, dn3 = up(up2), down(dn2)
    on_up = lax.rem(lax.axis_index("seq"), 2) == 0
    far = away(jnp.where(on_up, up3, dn3))
    by_off = {0: own, -1: up1, 1: dn1, -2: up2, 2: dn2, -3: up3, 3: dn3, 4: far}
    return [by_off[o] for o in OFFS]


def send_home(heads, outs, stats):
    at = {o: i for i, o in enumerate(OFFS)}
    core = lax.rem(lax.axis_index("seq"), 2).reshape(1).astype(jnp.int32)

    def loc(o):
        return outs[at[o]], stats[at[o]]

    far_o, far_s = away(outs[at[4]]), away(stats[at[4]])
    ou, su, od, sd = small_call(
        first_merge_kernel, heads, [core, far_o, far_s, *loc(3), *loc(-3)], 2, scalar=True
    )
    for o in (2, 1):
        ru_o, ru_s, rd_o, rd_s = up(ou), up(su), down(od), down(sd)
        ou, su, od, sd = small_call(
            merge_kernel, heads, [ru_o, ru_s, rd_o, rd_s, *loc(o), *loc(-o)], 2
        )
    ru_o, ru_s, rd_o, rd_s = up(ou), up(su), down(od), down(sd)
    return small_call(last_merge_kernel, heads, [ru_o, ru_s, rd_o, rd_s, *loc(0)], 0)


def routes(readers_of, me):
    blocks = jnp.stack([lax.rem(me + 4 * o + 32, 32) for o in OFFS]).astype(jnp.int32)
    tables, biases = [], []
    order = jnp.arange(HELD, dtype=jnp.int32)
    for pair in readers_of:
        picks, live = [], []
        for readers in pair:
            hit = jnp.any(readers[None, :, :] == blocks[:, None, None], axis=2)
            first = jnp.min(jnp.where(hit, order[None, :], HELD), axis=1)
            last = jnp.max(jnp.where(hit, order[None, :], -1), axis=1)
            picks += [jnp.minimum(first, HELD - 1), jnp.maximum(last, 0)]
            live += [last >= 0, last > first]
        tables.append(jnp.stack(picks, axis=1).astype(jnp.int32))
        alive = jnp.stack(live, axis=1)
        biases.append(jnp.repeat(jnp.where(alive, 0.0, NEG).astype(F32), PIECE, axis=1))
    return tables, biases


def weight_blocks(out_weight, core, y):
    mine, other = [], []
    for r in range(YS):
        target = lax.rem(y + r, YS)
        if r == 0:
            mine.append(lax.dynamic_slice_in_dim(out_weight, (core * YS + y) * 640, 640, 1))
            other.append(lax.dynamic_slice_in_dim(out_weight, ((1 - core) * YS + y) * 640, 640, 1))
        else:
            piece = lax.dynamic_slice_in_dim(out_weight, (core * YS + target) * 640, 640, 1)
            piece = head_move(piece, 0, r)
            mine.append(piece)
            other.append(swap_core(piece))
    return mine, other


def local(queries, cur_keys, cur_values, hist_keys, hist_values, piece_readers, out_weight):
    me = lax.axis_index("seq")
    core = lax.rem(me, 2)
    spot = lax.axis_index("head")
    y, x_hi = lax.rem(spot, YS), spot // YS
    readers_c = swap_core(piece_readers)
    readers_x = swap_x(piece_readers)
    readers_xc = swap_core(readers_x)
    tables, biases = routes(((piece_readers, readers_c), (readers_x, readers_xc)), me)
    mine, other = weight_blocks(out_weight, core, y)
    total_mine = total_other = None
    for h0, heads in CHUNKS:
        cols = slice(h0 * HDIM, (h0 + heads) * HDIM)
        own = jnp.concatenate(
            [cur_keys[:, cols], cur_values[:, cols], hist_keys[:, cols], hist_values[:, cols]], axis=0
        )
        own_x = swap_x(own)
        own_c = swap_core(own)
        own_xc = swap_core(own_x)
        asked = gather_queries(queries[:, cols])
        near = attend(heads, tables[0], biases[0], asked, (own, own_c), None)
        outs, stats = attend(heads, tables[1], biases[1], asked, (own_x, own_xc), near)
        attended = send_home(heads, outs, stats)
        for r in range(YS):
            part = attended if r == 0 else head_move(attended, 0, r)
            a = jnp.dot(part, mine[r][cols], preferred_element_type=F32)
            b = jnp.dot(part, other[r][cols], preferred_element_type=F32)
            total_mine = a if total_mine is None else total_mine + a
            total_other = b if total_other is None else total_other + b
    keeps = core == x_hi
    keep = jnp.where(keeps, total_mine, total_other)
    send = jnp.where(keeps, total_other, total_mine).astype(BF)
    return (keep + head_move(send, 1, 0).astype(F32)).astype(BF)


def solution(mesh):
    placed = (
        P("seq", "head"),
        P("seq", "head"),
        P("seq", "head"),
        P("seq", "head"),
        P("seq", "head"),
        P("seq", None),
        P("head", None),
    )
    return jax.shard_map(
        local, mesh=mesh, in_specs=placed, out_specs=P("seq", "head"), check_vma=False
    )
```

time: 660 us -> 197 us (0.30)
  waiting for transfers between devices: 515 us -> 90.4 us
  local copies, waits for them, and re-layouts: 54.7 us -> 15.3 us
  matrix products: 43.6 us -> 8.83 us
  Pallas kernels: 0 us -> 34.4 us
  starting transfers between devices: 20.7 us -> 45.3 us
  between operations: 13.6 us -> 0.24 us
  other arithmetic: 8.76 us -> 1.69 us
    ppermute x31 -> x37, waiting for transfers between devices: 298 us -> 90.4 us  [the longest x30 74.5 us: seq_move(): return lax.ppermute(value, 'seq', perm)]
    all_to_all x2 -> x0, waiting for transfers between devices: 115 us -> none  [the longest x1 115 us: local(): lax.all_to_all(outgoing, 'seq', split_axis=1, concat_axis=1, tiled=True)]
    unnamed x2 -> x0, waiting for transfers between devices: 102 us -> none
    ppermute x31 -> x37, starting transfers between devices: 2.56 us -> 45.3 us  [the longest x30 34.4 us: seq_move(): return lax.ppermute(value, 'seq', perm)]
    dot_general x68 -> x8, matrix products: 43.6 us -> 8.83 us  [the longest x4 6.13 us: local(): a = jnp.dot(part, mine[r][cols], preferred_element_type=F32)]
    pallas_call x0 -> x6, Pallas kernels: none -> 34.4 us  [the longest x2 31.6 us: attend(): pl.pallas_call(functools.partial(attend_kernel, heads, first), out_shape=...]
    slice x94 -> x0, local copies, waits for them, and re-layouts: 21 us -> none  [the longest x63 15.4 us: attend(): val_heads = key_val[1].reshape(-1, head_count, HDIM)]
    all_to_all x2 -> x0, starting transfers between devices: 18.1 us -> none  [the longest x1 9.65 us: local(): lax.all_to_all(slot_full, 'seq', split_axis=1, concat_axis=1, tiled=True)]
  transfers between devices with their start and end apart: 34 -> 37, of which waited for: 33 -> 21; matrix products, arithmetic and copies ran while one was open for 3% -> 7% of each run, Pallas kernels for 0% -> 9%
where the time goes in v1:
time: 197 us; the launch traced here: 196 us
  waiting for transfers between devices  90.4 us (46%)
  starting transfers between devices  45.3 us (23%)
  Pallas kernels  34.4 us (17%)
  local copies, waits for them, and re-layouts  15.3 us (8%)
  matrix products  8.83 us (4%)
    ppermute x30, waiting for transfers between devices, seq_move(): return lax.ppermute(value, 'seq', perm)  74.5 us
    ppermute x30, starting transfers between devices, seq_move(): return lax.ppermute(value, 'seq', perm)  34.4 us
    pallas_call x2, Pallas kernels, attend(): pl.pallas_call(functools.partial(attend_kernel, heads, first), out_shape=...  31.6 us
    ppermute x7, waiting for transfers between devices, head_move(): return lax.ppermute(value, 'head', perm)  15.8 us
    ppermute x7, starting transfers between devices, head_move(): return lax.ppermute(value, 'head', perm)  10.9 us
    unnamed x23, local copies, waits for them, and re-layouts  9.97 us
    dot_general x4, matrix products, local(): a = jnp.dot(part, mine[r][cols], preferred_element_type=F32)  6.13 us
  transfers between devices with their start and end apart: 37, of which 21 were waited for; matrix products, arithmetic and copies ran while one was open for 7% of the time, Pallas kernels for 9%

profile of v1, /device:TPU:32, one launch (start us, length us, event | category | flops | bytes accessed | tf_op | source)
XLA Modules:
  0.0 196.2 jit_solution(5428256063280551033)
XLA Ops:
  0.0 1.7 constant_dynamic-update-slice_fusion.3
  1.8 1.7 constant_dynamic-update-slice_fusion.2
  3.4 1.9 constant_dynamic-update-slice_fusion.1
  5.3 0.9 constant_dynamic-update-slice_fusion.refs_10_
  6.2 1.5 collective-permute-start.9
  8.2 1.9 collective-permute-start.2
  10.4 33.7 %collective-permute-done = s32[14,2]{0,1:T(2,128)S(1)} collective-permute-done((s32[14,2]{0,1:T(2,128)S(1)}, s32[14,2]{0,1:T(2,128)S(1)}, u32[]{:S(2)}, u32[]{:S(2)}) %collective-permute-start) | collective-permute-done | bytes 144 | tf_op jit(solution)/shard_map/ppermute | solution.py:37
  46.3 1.9 collective-permute-start.3
  48.3 6.1 %collective-permute-done.3.refs_6_ = bf16[192,640]{1,0:T(8,128)(2,1)S(1)} collective-permute-done((bf16[192,640]{1,0:T(8,128)(2,1)S(1)}, bf16[192,640]{1,0:T(8,128)(2,1)S(1)}, u32[]{:S(2)}, u32[]{:S(2)}) %collective-permute-start.3) | collective-permute-done | bytes 245792 | tf_op jit(solution)/shard_map/ppermute | solution.py:37
  54.4 1.9 collective-permute-start.4
  56.4 2.3 %collective-permute-start.7 = (bf16[192,640]{1,0:T(8,128)(2,1)S(1)}, bf16[192,640]{1,0:T(8,128)(2,1)S(1)}, u32[]{:S(2)}, u32[]{:S(2)}) collective-permute-start(bf16[192,640]{1,0:T(8,128)(2,1)S(1)} %collective-permute-done.6.refs_5_), channel_id=1, source_target_pairs={{0,224},{8,232},{16,240},{24,248},{32,0},{40,8},{48,16},{56,24},{6... | collective-permute-start | bytes 737288 | tf_op jit(solution)/shard_map/ppermute | solution.py:37
  58.7 5.9 %collective-permute-done.4.refs_4_ = bf16[192,640]{1,0:T(8,128)(2,1)S(1)} collective-permute-done((bf16[192,640]{1,0:T(8,128)(2,1)S(1)}, bf16[192,640]{1,0:T(8,128)(2,1)S(1)}, u32[]{:S(2)}, u32[]{:S(2)}) %collective-permute-start.4) | collective-permute-done | bytes 245792 | tf_op jit(solution)/shard_map/ppermute | solution.py:37
  65.0 3.2 %collective-permute-start.8 = (bf16[192,640]{1,0:T(8,128)(2,1)S(1)}, bf16[192,640]{1,0:T(8,128)(2,1)S(1)}, u32[]{:S(2)}, u32[]{:S(2)}) collective-permute-start(bf16[192,640]{1,0:T(8,128)(2,1)S(1)} %broadcast_select_fusion), channel_id=1, source_target_pairs={{0,32},{8,232},{16,48},{24,248},{32,64},{40,8},{48,80},{56,24},{64... | collective-permute-start | bytes 737288 | tf_op jit(solution)/shard_map/ppermute | solution.py:37
  69.6 2.5 %collective-permute-done.8.refs_2_ = bf16[192,640]{1,0:T(8,128)(2,1)S(1)} collective-permute-done((bf16[192,640]{1,0:T(8,128)(2,1)S(1)}, bf16[192,640]{1,0:T(8,128)(2,1)S(1)}, u32[]{:S(2)}, u32[]{:S(2)}) %collective-permute-start.8) | collective-permute-done | bytes 245792 | tf_op jit(solution)/shard_map/ppermute | solution.py:37
  72.0 15.1 %shard_map.73 = (f32[192,640]{1,0:T(8,128)S(1)}, f32[192,640]{1,0:T(8,128)S(1)}, f32[192,640]{1,0:T(8,128)S(1)}, f32[192,640]{1,0:T(8,128)S(1)}, f32[192,640]{1,...) custom-call(s32[8,4]{1,0:T(8,128)S(1)} %pad_add_fusion.1.refs_0_, ...), custom_call_target="tpu_custom_call" | custom-call | flops 2013265920 | bytes 5898240 | tf_op jit(solution)/shard_map/pallas_call | solution.py:142
  91.0 16.5 %shard_map.74 = (bf16[192,640]{1,0:T(8,128)(2,1)}, bf16[192,640]{1,0:T(8,128)(2,1)S(1)}, bf16[192,640]{1,0:T(8,128)(2,1)S(1)}, bf16[192,640]{1,0:T(8,128)(2,1)S(...) custom-call(s32[8,4]{1,0:T(8,128)S(1)} %pad_add_fusion.refs_0_, ...), custom_call_target="tpu_custom_call" | custom-call | flops 2013265920 | bytes 5898240 | tf_op jit(solution)/shard_map/pallas_call | solution.py:142
  108.3 2.9 %collective-permute-start.13 = (bf16[192,640]{1,0:T(8,128)(2,1)}, bf16[192,640]{1,0:T(8,128)(2,1)S(1)}, u32[]{:S(2)}, u32[]{:S(2)}) collective-permute-start(bf16[192,640]{1,0:T(8,128)(2,1)} %get-tuple-element.65), channel_id=1, source_target_pairs={{0,32},{8,232},{16,48},{24,248},{32,64},{40,8},{48,80},{56,24},{64... | collective-permute-start | bytes 737288 | tf_op jit(solution)/shard_map/ppermute | solution.py:37
  111.2 3.2 %constant_dynamic-slice_fusion.1 = (bf16[640,640]{1,0:T(8,128)(2,1)}, bf16[640,640]{1,0:T(8,128)(2,1)}, bf16[640,640]{1,0:T(8,128)(2,1)}) fusion(bf16[640,5120]{1,0:T(8,128)(2,1)} %param.13, s32[]{:T(128)S(6)} %select_n.88, s32[]{:T(128)S(6)} %select_n.87, s32[]{:T(128)S(6)} %select_n.89), kind=kLoop, calls=%fused_computation.42 | loop fusion | bytes 4915212 | tf_op jit(solution)/shard_map/dynamic_slice | solution.py:276
  114.4 1.6 collective-permute-start.28
  116.0 1.7 collective-permute-start.32
  117.7 2.0 %collective-permute-start.30 = (bf16[640,640]{1,0:T(8,128)(2,1)}, bf16[640,640]{1,0:T(8,128)(2,1)}, u32[]{:S(2)}, u32[]{:S(2)}) collective-permute-start(bf16[640,640]{1,0:T(8,128)(2,1)} %get-tuple-element.105), channel_id=1, source_target_pairs={{0,2},{1,3},{2,0},{3,1},{4,6},{5,7},{6,4},{7,5},{8,10},{9,11},{10,... | collective-permute-start | bytes 2457608 | tf_op jit(solution)/shard_map/ppermute | solution.py:65
  119.7 2.5 %collective-permute-start.14 = (f32[8,256]{1,0:T(8,128)S(1)}, f32[8,256]{1,0:T(8,128)S(1)}, u32[]{:S(2)}, u32[]{:S(2)}) collective-permute-start(f32[8,256]{1,0:T(8,128)S(1)} %get-tuple-element.66), channel_id=1, source_target_pairs={{0,32},{8,232},{16,48},{24,248},{32,64},{40,8},{48,80},{56,24},{64... | collective-permute-start | bytes 24584 | tf_op jit(solution)/shard_map/ppermute | solution.py:37
  122.2 1.4 collective-permute-done.14.far_s
  124.3 2.4 %collective-permute-start.16 = (f32[8,256]{1,0:T(8,128)S(1)}, f32[8,256]{1,0:T(8,128)S(1)}, u32[]{:S(2)}, u32[]{:S(2)}) collective-permute-start(f32[8,256]{1,0:T(8,128)S(1)} %get-tuple-element.72), channel_id=1, source_target_pairs={{0,32},{8,40},{16,48},{24,56},{32,64},{40,72},{48,80},{56,88},{64,... | collective-permute-start | bytes 24584 | tf_op jit(solution)/shard_map/ppermute | solution.py:37
  126.7 1.4 collective-permute-done.16.ru_s
  128.1 2.4 %collective-permute-start.15 = (bf16[192,640]{1,0:T(8,128)(2,1)S(1)}, bf16[192,640]{1,0:T(8,128)(2,1)S(1)}, u32[]{:S(2)}, u32[]{:S(2)}) collective-permute-start(bf16[192,640]{1,0:T(8,128)(2,1)S(1)} %get-tuple-element.71), channel_id=1, source_target_pairs={{0,32},{8,40},{16,48},{24,56},{32,64},{40,72},{48,80},{56,88},{64,... | collective-permute-start | bytes 737288 | tf_op jit(solution)/shard_map/ppermute | solution.py:37
  130.6 4.2 %collective-permute-done.15.ru_o = bf16[192,640]{1,0:T(8,128)(2,1)S(1)} collective-permute-done((bf16[192,640]{1,0:T(8,128)(2,1)S(1)}, bf16[192,640]{1,0:T(8,128)(2,1)S(1)}, u32[]{:S(2)}, u32[]{:S(2)}) %collective-permute-start.15) | collective-permute-done | bytes 245792 | tf_op jit(solution)/shard_map/ppermute | solution.py:37
  134.8 1.9 collective-permute-done.17.rd_o
  137.4 1.9 collective-permute-start.20
  139.5 1.8 collective-permute-done.20.ru_s
  141.3 2.6 %collective-permute-start.19 = (bf16[192,640]{1,0:T(8,128)(2,1)S(1)}, bf16[192,640]{1,0:T(8,128)(2,1)S(1)}, u32[]{:S(2)}, u32[]{:S(2)}) collective-permute-start(bf16[192,640]{1,0:T(8,128)(2,1)S(1)} %get-tuple-element.79), channel_id=1, source_target_pairs={{0,32},{8,40},{16,48},{24,56},{32,64},{40,72},{48,80},{56,88},{64,... | collective-permute-start | bytes 737288 | tf_op jit(solution)/shard_map/ppermute | solution.py:37
  144.2 4.0 %collective-permute-done.19.ru_o = bf16[192,640]{1,0:T(8,128)(2,1)S(1)} collective-permute-done((bf16[192,640]{1,0:T(8,128)(2,1)S(1)}, bf16[192,640]{1,0:T(8,128)(2,1)S(1)}, u32[]{:S(2)}, u32[]{:S(2)}) %collective-permute-start.19) | collective-permute-done | bytes 245792 | tf_op jit(solution)/shard_map/ppermute | solution.py:37
  148.1 2.3 %collective-permute-done.21.rd_o = bf16[192,640]{1,0:T(8,128)(2,1)S(1)} collective-permute-done((bf16[192,640]{1,0:T(8,128)(2,1)S(1)}, bf16[192,640]{1,0:T(8,128)(2,1)S(1)}, u32[]{:S(2)}, u32[]{:S(2)}) %collective-permute-start.21) | collective-permute-done | bytes 245792 | tf_op jit(solution)/shard_map/ppermute | solution.py:37
  151.2 2.1 %collective-permute-start.24 = (f32[8,256]{1,0:T(8,128)S(1)}, f32[8,256]{1,0:T(8,128)S(1)}, u32[]{:S(2)}, u32[]{:S(2)}) collective-permute-start(f32[8,256]{1,0:T(8,128)S(1)} %get-tuple-element.88), channel_id=1, source_target_pairs={{0,32},{8,40},{16,48},{24,56},{32,64},{40,72},{48,80},{56,88},{64,... | collective-permute-start | bytes 24584 | tf_op jit(solution)/shard_map/ppermute | solution.py:37
  153.3 1.6 collective-permute-done.24.ru_s
  154.9 2.4 %collective-permute-start.23 = (bf16[192,640]{1,0:T(8,128)(2,1)S(1)}, bf16[192,640]{1,0:T(8,128)(2,1)S(1)}, u32[]{:S(2)}, u32[]{:S(2)}) collective-permute-start(bf16[192,640]{1,0:T(8,128)(2,1)S(1)} %get-tuple-element.87), channel_id=1, source_target_pairs={{0,32},{8,40},{16,48},{24,56},{32,64},{40,72},{48,80},{56,88},{64,... | collective-permute-start | bytes 737288 | tf_op jit(solution)/shard_map/ppermute | solution.py:37
  157.6 3.7 %collective-permute-done.23.ru_o = bf16[192,640]{1,0:T(8,128)(2,1)S(1)} collective-permute-done((bf16[192,640]{1,0:T(8,128)(2,1)S(1)}, bf16[192,640]{1,0:T(8,128)(2,1)S(1)}, u32[]{:S(2)}, u32[]{:S(2)}) %collective-permute-start.23) | collective-permute-done | bytes 245792 | tf_op jit(solution)/shard_map/ppermute | solution.py:37
  161.3 2.5 %collective-permute-done.25.rd_o = bf16[192,640]{1,0:T(8,128)(2,1)S(1)} collective-permute-done((bf16[192,640]{1,0:T(8,128)(2,1)S(1)}, bf16[192,640]{1,0:T(8,128)(2,1)S(1)}, u32[]{:S(2)}, u32[]{:S(2)}) %collective-permute-start.25) | collective-permute-done | bytes 245792 | tf_op jit(solution)/shard_map/ppermute | solution.py:37
  165.8 1.7 collective-permute-start.29
  167.6 1.5 fusion.3
  169.1 8.0 %collective-permute-done.27 = bf16[192,640]{1,0:T(8,128)(2,1)S(1)} collective-permute-done((bf16[192,640]{1,0:T(8,128)(2,1)S(1)}, bf16[192,640]{1,0:T(8,128)(2,1)S(1)}, u32[]{:S(2)}, u32[]{:S(2)}) %collective-permute-start.27) | collective-permute-done | bytes 245792 | tf_op jit(solution)/shard_map/ppermute | solution.py:65
  177.1 1.5 fusion.8
  178.7 1.5 fusion.9
  180.2 3.1 %collective-permute-done.31 = bf16[192,640]{1,0:T(8,128)(2,1)S(1)} collective-permute-done((bf16[192,640]{1,0:T(8,128)(2,1)S(1)}, bf16[192,640]{1,0:T(8,128)(2,1)S(1)}, u32[]{:S(2)}, u32[]{:S(2)}) %collective-permute-start.31) | collective-permute-done | bytes 245792 | tf_op jit(solution)/shard_map/ppermute | solution.py:65
  183.3 1.5 fusion.10
  185.7 1.5 fusion.2
  187.6 3.1 %collective-permute-start.36 = (bf16[192,640]{1,0:T(8,128)(2,1)S(1)}, bf16[192,640]{1,0:T(8,128)(2,1)S(1)}, u32[]{:S(2)}, u32[]{:S(2)}) collective-permute-start(bf16[192,640]{1,0:T(8,128)(2,1)S(1)} %get-tuple-element.116), channel_id=1, source_target_pairs={{0,4},{1,5},{2,6},{3,7},{4,0},{5,1},{6,2},{7,3},{8,12},{9,13},{10,... | collective-permute-start | bytes 737288 | tf_op jit(solution)/shard_map/ppermute | solution.py:65
  190.7 4.7 %collective-permute-done.36 = bf16[192,640]{1,0:T(8,128)(2,1)S(1)} collective-permute-done((bf16[192,640]{1,0:T(8,128)(2,1)S(1)}, bf16[192,640]{1,0:T(8,128)(2,1)S(1)}, u32[]{:S(2)}, u32[]{:S(2)}) %collective-permute-start.36) | collective-permute-done | bytes 245792 | tf_op jit(solution)/shard_map/ppermute | solution.py:65
  (99 shorter events, 16.5 us)
Async XLA Ops:
  0.0 5.3 %copy-start.8 = (bf16[448,640]{1,0:T(8,128)(2,1)S(1)}, bf16[448,640]{1,0:T(8,128)(2,1)}, u32[]{:S(2)}) copy-start(bf16[448,640]{1,0:T(8,128)(2,1)} %param.11) | copy-start | bytes 1720324
  0.0 7.7 %copy-start.9 = (s32[14,2]{0,1:T(2,128)S(1)}, s32[14,2]{0,1:T(2,128)}, u32[]{:S(2)}) copy-start(s32[14,2]{0,1:T(2,128)} %param.12) | copy-start | bytes 340
  0.0 8.2 %copy-start.5 = (bf16[192,640]{1,0:T(8,128)(2,1)S(1)}, bf16[192,640]{1,0:T(8,128)(2,1)}, u32[]{:S(2)}) copy-start(bf16[192,640]{1,0:T(8,128)(2,1)} %refs_9_.3) | copy-start | bytes 737284
  6.2 39.7 %collective-permute-start.9 = (bf16[1280,640]{1,0:T(8,128)(2,1)}, bf16[1280,640]{1,0:T(8,128)(2,1)}, u32[]{:S(2)}, u32[]{:S(2)}) collective-permute-start(bf16[1280,640]{1,0:T(8,128)(2,1)} %constant_dynamic-update-slice_fusion.refs_10_), channel_id=1, source_target_pairs={{0,16},{8,24},{16,0},{24,8},{32,48},{40,56},{48,32},{56,40},{64,80... | collective-permute-start | bytes 4915208 | tf_op jit(solution)/shard_map/ppermute | solution.py:37
  7.7 36.4 %collective-permute-start = (s32[14,2]{0,1:T(2,128)S(1)}, s32[14,2]{0,1:T(2,128)S(1)}, u32[]{:S(2)}, u32[]{:S(2)}) collective-permute-start(s32[14,2]{0,1:T(2,128)S(1)} %copy-done.9), channel_id=1, source_target_pairs={{0,16},{8,24},{16,0},{24,8},{32,48},{40,56},{48,32},{56,40},{64,80... | collective-permute-start | bytes 344 | tf_op jit(solution)/shard_map/ppermute | solution.py:37
  8.2 35.8 %collective-permute-start.11 = (s32[14,2]{0,1:T(2,128)S(1)}, s32[14,2]{0,1:T(2,128)S(1)}, u32[]{:S(2)}, u32[]{:S(2)}) collective-permute-start(s32[14,2]{0,1:T(2,128)S(1)} %copy-done.9), channel_id=1, source_target_pairs={{0,8},{8,0},{16,24},{24,16},{32,40},{40,32},{48,56},{56,48},{64,72... | collective-permute-start | bytes 344 | tf_op jit(solution)/shard_map/ppermute | solution.py:37
  8.2 38.0 %collective-permute-start.2 = (bf16[192,640]{1,0:T(8,128)(2,1)S(1)}, bf16[192,640]{1,0:T(8,128)(2,1)S(1)}, u32[]{:S(2)}, u32[]{:S(2)}) collective-permute-start(bf16[192,640]{1,0:T(8,128)(2,1)S(1)} %copy-done.5), channel_id=1, source_target_pairs={{0,32},{8,40},{16,48},{24,56},{32,64},{40,72},{48,80},{56,88},{64,... | collective-permute-start | bytes 737288 | tf_op jit(solution)/shard_map/ppermute | solution.py:37
  10.2 38.0 %collective-permute-start.5 = (bf16[192,640]{1,0:T(8,128)(2,1)S(1)}, bf16[192,640]{1,0:T(8,128)(2,1)S(1)}, u32[]{:S(2)}, u32[]{:S(2)}) collective-permute-start(bf16[192,640]{1,0:T(8,128)(2,1)S(1)} %copy-done.5), channel_id=1, source_target_pairs={{0,224},{8,232},{16,240},{24,248},{32,0},{40,8},{48,16},{56,24},{6... | collective-permute-start | bytes 737288 | tf_op jit(solution)/shard_map/ppermute | solution.py:37
  44.1 1.1 collective-permute-start.1
  44.1 27.9 %collective-permute-start.12 = (bf16[1280,640]{1,0:T(8,128)(2,1)}, bf16[1280,640]{1,0:T(8,128)(2,1)}, u32[]{:S(2)}, u32[]{:S(2)}) collective-permute-start(bf16[1280,640]{1,0:T(8,128)(2,1)} %constant_dynamic-update-slice_fusion.refs_10_), channel_id=1, source_target_pairs={{0,8},{8,0},{16,24},{24,16},{32,40},{40,32},{48,56},{56,48},{64,72... | collective-permute-start | bytes 4915208 | tf_op jit(solution)/shard_map/ppermute | solution.py:37
  46.0 45.1 %collective-permute-start.10 = (bf16[1280,640]{1,0:T(8,128)(2,1)}, bf16[1280,640]{1,0:T(8,128)(2,1)}, u32[]{:S(2)}, u32[]{:S(2)}) collective-permute-start(bf16[1280,640]{1,0:T(8,128)(2,1)} %collective-permute-done.9.refs_10_), channel_id=1, source_target_pairs={{0,8},{8,0},{16,24},{24,16},{32,40},{40,32},{48,56},{56,48},{64,72... | collective-permute-start | bytes 4915208 | tf_op jit(solution)/shard_map/ppermute | solution.py:37
  46.3 8.2 %collective-permute-start.3 = (bf16[192,640]{1,0:T(8,128)(2,1)S(1)}, bf16[192,640]{1,0:T(8,128)(2,1)S(1)}, u32[]{:S(2)}, u32[]{:S(2)}) collective-permute-start(bf16[192,640]{1,0:T(8,128)(2,1)S(1)} %collective-permute-done.2.refs_8_), channel_id=1, source_target_pairs={{0,32},{8,40},{16,48},{24,56},{32,64},{40,72},{48,80},{56,88},{64,... | collective-permute-start | bytes 737288 | tf_op jit(solution)/shard_map/ppermute | solution.py:37
  48.2 8.2 %collective-permute-start.6 = (bf16[192,640]{1,0:T(8,128)(2,1)S(1)}, bf16[192,640]{1,0:T(8,128)(2,1)S(1)}, u32[]{:S(2)}, u32[]{:S(2)}) collective-permute-start(bf16[192,640]{1,0:T(8,128)(2,1)S(1)} %collective-permute-done.5.refs_7_), channel_id=1, source_target_pairs={{0,224},{8,232},{16,240},{24,248},{32,0},{40,8},{48,16},{56,24},{6... | collective-permute-start | bytes 737288 | tf_op jit(solution)/shard_map/ppermute | solution.py:37
  54.4 10.2 %collective-permute-start.4 = (bf16[192,640]{1,0:T(8,128)(2,1)S(1)}, bf16[192,640]{1,0:T(8,128)(2,1)S(1)}, u32[]{:S(2)}, u32[]{:S(2)}) collective-permute-start(bf16[192,640]{1,0:T(8,128)(2,1)S(1)} %collective-permute-done.3.refs_6_), channel_id=1, source_target_pairs={{0,32},{8,40},{16,48},{24,56},{32,64},{40,72},{48,80},{56,88},{64,... | collective-permute-start | bytes 737288 | tf_op jit(solution)/shard_map/ppermute | solution.py:37
  56.4 8.7 %collective-permute-start.7 = (bf16[192,640]{1,0:T(8,128)(2,1)S(1)}, bf16[192,640]{1,0:T(8,128)(2,1)S(1)}, u32[]{:S(2)}, u32[]{:S(2)}) collective-permute-start(bf16[192,640]{1,0:T(8,128)(2,1)S(1)} %collective-permute-done.6.refs_5_), channel_id=1, source_target_pairs={{0,224},{8,232},{16,240},{24,248},{32,0},{40,8},{48,16},{56,24},{6... | collective-permute-start | bytes 737288 | tf_op jit(solution)/shard_map/ppermute | solution.py:37
  65.0 7.0 %collective-permute-start.8 = (bf16[192,640]{1,0:T(8,128)(2,1)S(1)}, bf16[192,640]{1,0:T(8,128)(2,1)S(1)}, u32[]{:S(2)}, u32[]{:S(2)}) collective-permute-start(bf16[192,640]{1,0:T(8,128)(2,1)S(1)} %broadcast_select_fusion), channel_id=1, source_target_pairs={{0,32},{8,232},{16,48},{24,248},{32,64},{40,8},{48,80},{56,24},{64... | collective-permute-start | bytes 737288 | tf_op jit(solution)/shard_map/ppermute | solution.py:37
  87.1 0.8 copy-start
  87.9 0.8 copy-start.1
  88.7 0.8 copy-start.2
  89.5 0.8 copy-start.3
  90.3 0.8 copy-start.4
  107.6 0.7 copy-start.6
  108.3 15.3 %collective-permute-start.13 = (bf16[192,640]{1,0:T(8,128)(2,1)}, bf16[192,640]{1,0:T(8,128)(2,1)S(1)}, u32[]{:S(2)}, u32[]{:S(2)}) collective-permute-start(bf16[192,640]{1,0:T(8,128)(2,1)} %get-tuple-element.65), channel_id=1, source_target_pairs={{0,32},{8,232},{16,48},{24,248},{32,64},{40,8},{48,80},{56,24},{64... | collective-permute-start | bytes 737288 | tf_op jit(solution)/shard_map/ppermute | solution.py:37
  111.2 12.3 %copy-start.7 = (bf16[192,640]{1,0:T(8,128)(2,1)S(1)}, bf16[192,640]{1,0:T(8,128)(2,1)}, u32[]{:S(2)}) copy-start(bf16[192,640]{1,0:T(8,128)(2,1)} %copy-done.6) | copy-start | bytes 737284
  114.4 50.8 %collective-permute-start.28 = (bf16[640,640]{1,0:T(8,128)(2,1)}, bf16[640,640]{1,0:T(8,128)(2,1)}, u32[]{:S(2)}, u32[]{:S(2)}) collective-permute-start(bf16[640,640]{1,0:T(8,128)(2,1)} %get-tuple-element.106), channel_id=1, source_target_pairs={{0,1},{1,2},{2,3},{3,0},{4,5},{5,6},{6,7},{7,4},{8,9},{9,10},{10,1... | collective-permute-start | bytes 2457608 | tf_op jit(solution)/shard_map/ppermute | solution.py:65
  116.0 49.2 %collective-permute-start.32 = (bf16[640,640]{1,0:T(8,128)(2,1)}, bf16[640,640]{1,0:T(8,128)(2,1)}, u32[]{:S(2)}, u32[]{:S(2)}) collective-permute-start(bf16[640,640]{1,0:T(8,128)(2,1)} %get-tuple-element.107), channel_id=1, source_target_pairs={{0,3},{1,0},{2,1},{3,2},{4,7},{5,4},{6,5},{7,6},{8,11},{9,8},{10,9... | collective-permute-start | bytes 2457608 | tf_op jit(solution)/shard_map/ppermute | solution.py:65
  117.7 48.1 %collective-permute-start.30 = (bf16[640,640]{1,0:T(8,128)(2,1)}, bf16[640,640]{1,0:T(8,128)(2,1)}, u32[]{:S(2)}, u32[]{:S(2)}) collective-permute-start(bf16[640,640]{1,0:T(8,128)(2,1)} %get-tuple-element.105), channel_id=1, source_target_pairs={{0,2},{1,3},{2,0},{3,1},{4,6},{5,7},{6,4},{7,5},{8,10},{9,11},{10,... | collective-permute-start | bytes 2457608 | tf_op jit(solution)/shard_map/ppermute | solution.py:65
  119.7 3.9 %collective-permute-start.14 = (f32[8,256]{1,0:T(8,128)S(1)}, f32[8,256]{1,0:T(8,128)S(1)}, u32[]{:S(2)}, u32[]{:S(2)}) collective-permute-start(f32[8,256]{1,0:T(8,128)S(1)} %get-tuple-element.66), channel_id=1, source_target_pairs={{0,32},{8,232},{16,48},{24,248},{32,64},{40,8},{48,80},{56,24},{64... | collective-permute-start | bytes 24584 | tf_op jit(solution)/shard_map/ppermute | solution.py:37
  124.3 3.8 %collective-permute-start.16 = (f32[8,256]{1,0:T(8,128)S(1)}, f32[8,256]{1,0:T(8,128)S(1)}, u32[]{:S(2)}, u32[]{:S(2)}) collective-permute-start(f32[8,256]{1,0:T(8,128)S(1)} %get-tuple-element.72), channel_id=1, source_target_pairs={{0,32},{8,40},{16,48},{24,56},{32,64},{40,72},{48,80},{56,88},{64,... | collective-permute-start | bytes 24584 | tf_op jit(solution)/shard_map/ppermute | solution.py:37
  126.7 3.8 %collective-permute-start.18 = (f32[8,256]{1,0:T(8,128)S(1)}, f32[8,256]{1,0:T(8,128)S(1)}, u32[]{:S(2)}, u32[]{:S(2)}) collective-permute-start(f32[8,256]{1,0:T(8,128)S(1)} %get-tuple-element.74), channel_id=1, source_target_pairs={{0,224},{8,232},{16,240},{24,248},{32,0},{40,8},{48,16},{56,24},{6... | collective-permute-start | bytes 24584 | tf_op jit(solution)/shard_map/ppermute | solution.py:37
  128.1 6.7 %collective-permute-start.15 = (bf16[192,640]{1,0:T(8,128)(2,1)S(1)}, bf16[192,640]{1,0:T(8,128)(2,1)S(1)}, u32[]{:S(2)}, u32[]{:S(2)}) collective-permute-start(bf16[192,640]{1,0:T(8,128)(2,1)S(1)} %get-tuple-element.71), channel_id=1, source_target_pairs={{0,32},{8,40},{16,48},{24,56},{32,64},{40,72},{48,80},{56,88},{64,... | collective-permute-start | bytes 737288 | tf_op jit(solution)/shard_map/ppermute | solution.py:37
  130.5 6.2 %collective-permute-start.17 = (bf16[192,640]{1,0:T(8,128)(2,1)S(1)}, bf16[192,640]{1,0:T(8,128)(2,1)S(1)}, u32[]{:S(2)}, u32[]{:S(2)}) collective-permute-start(bf16[192,640]{1,0:T(8,128)(2,1)S(1)} %get-tuple-element.73), channel_id=1, source_target_pairs={{0,224},{8,232},{16,240},{24,248},{32,0},{40,8},{48,16},{56,24},{6... | collective-permute-start | bytes 737288 | tf_op jit(solution)/shard_map/ppermute | solution.py:37
  137.4 3.9 %collective-permute-start.20 = (f32[8,256]{1,0:T(8,128)S(1)}, f32[8,256]{1,0:T(8,128)S(1)}, u32[]{:S(2)}, u32[]{:S(2)}) collective-permute-start(f32[8,256]{1,0:T(8,128)S(1)} %get-tuple-element.80), channel_id=1, source_target_pairs={{0,32},{8,40},{16,48},{24,56},{32,64},{40,72},{48,80},{56,88},{64,... | collective-permute-start | bytes 24584 | tf_op jit(solution)/shard_map/ppermute | solution.py:37
  139.3 4.9 %collective-permute-start.22 = (f32[8,256]{1,0:T(8,128)S(1)}, f32[8,256]{1,0:T(8,128)S(1)}, u32[]{:S(2)}, u32[]{:S(2)}) collective-permute-start(f32[8,256]{1,0:T(8,128)S(1)} %get-tuple-element.82), channel_id=1, source_target_pairs={{0,224},{8,232},{16,240},{24,248},{32,0},{40,8},{48,16},{56,24},{6... | collective-permute-start | bytes 24584 | tf_op jit(solution)/shard_map/ppermute | solution.py:37
  141.3 6.8 %collective-permute-start.19 = (bf16[192,640]{1,0:T(8,128)(2,1)S(1)}, bf16[192,640]{1,0:T(8,128)(2,1)S(1)}, u32[]{:S(2)}, u32[]{:S(2)}) collective-permute-start(bf16[192,640]{1,0:T(8,128)(2,1)S(1)} %get-tuple-element.79), channel_id=1, source_target_pairs={{0,32},{8,40},{16,48},{24,56},{32,64},{40,72},{48,80},{56,88},{64,... | collective-permute-start | bytes 737288 | tf_op jit(solution)/shard_map/ppermute | solution.py:37
  144.1 6.3 %collective-permute-start.21 = (bf16[192,640]{1,0:T(8,128)(2,1)S(1)}, bf16[192,640]{1,0:T(8,128)(2,1)S(1)}, u32[]{:S(2)}, u32[]{:S(2)}) collective-permute-start(bf16[192,640]{1,0:T(8,128)(2,1)S(1)} %get-tuple-element.81), channel_id=1, source_target_pairs={{0,224},{8,232},{16,240},{24,248},{32,0},{40,8},{48,16},{56,24},{6... | collective-permute-start | bytes 737288 | tf_op jit(solution)/shard_map/ppermute | solution.py:37
  151.2 3.7 %collective-permute-start.24 = (f32[8,256]{1,0:T(8,128)S(1)}, f32[8,256]{1,0:T(8,128)S(1)}, u32[]{:S(2)}, u32[]{:S(2)}) collective-permute-start(f32[8,256]{1,0:T(8,128)S(1)} %get-tuple-element.88), channel_id=1, source_target_pairs={{0,32},{8,40},{16,48},{24,56},{32,64},{40,72},{48,80},{56,88},{64,... | collective-permute-start | bytes 24584 | tf_op jit(solution)/shard_map/ppermute | solution.py:37
  153.3 4.3 %collective-permute-start.26 = (f32[8,256]{1,0:T(8,128)S(1)}, f32[8,256]{1,0:T(8,128)S(1)}, u32[]{:S(2)}, u32[]{:S(2)}) collective-permute-start(f32[8,256]{1,0:T(8,128)S(1)} %get-tuple-element.90), channel_id=1, source_target_pairs={{0,224},{8,232},{16,240},{24,248},{32,0},{40,8},{48,16},{56,24},{6... | collective-permute-start | bytes 24584 | tf_op jit(solution)/shard_map/ppermute | solution.py:37
  154.9 6.4 %collective-permute-start.23 = (bf16[192,640]{1,0:T(8,128)(2,1)S(1)}, bf16[192,640]{1,0:T(8,128)(2,1)S(1)}, u32[]{:S(2)}, u32[]{:S(2)}) collective-permute-start(bf16[192,640]{1,0:T(8,128)(2,1)S(1)} %get-tuple-element.87), channel_id=1, source_target_pairs={{0,32},{8,40},{16,48},{24,56},{32,64},{40,72},{48,80},{56,88},{64,... | collective-permute-start | bytes 737288 | tf_op jit(solution)/shard_map/ppermute | solution.py:37
  157.6 6.2 %collective-permute-start.25 = (bf16[192,640]{1,0:T(8,128)(2,1)S(1)}, bf16[192,640]{1,0:T(8,128)(2,1)S(1)}, u32[]{:S(2)}, u32[]{:S(2)}) collective-permute-start(bf16[192,640]{1,0:T(8,128)(2,1)S(1)} %get-tuple-element.89), channel_id=1, source_target_pairs={{0,224},{8,232},{16,240},{24,248},{32,0},{40,8},{48,16},{56,24},{6... | collective-permute-start | bytes 737288 | tf_op jit(solution)/shard_map/ppermute | solution.py:37
  164.4 12.8 %collective-permute-start.27 = (bf16[192,640]{1,0:T(8,128)(2,1)S(1)}, bf16[192,640]{1,0:T(8,128)(2,1)S(1)}, u32[]{:S(2)}, u32[]{:S(2)}) collective-permute-start(bf16[192,640]{1,0:T(8,128)(2,1)S(1)} %shard_map.78), channel_id=1, source_target_pairs={{0,1},{1,2},{2,3},{3,0},{4,5},{5,6},{6,7},{7,4},{8,9},{9,10},{10,1... | collective-permute-start | bytes 737288 | tf_op jit(solution)/shard_map/ppermute | solution.py:65
  165.2 20.0 %collective-permute-start.33 = (bf16[640,640]{1,0:T(8,128)(2,1)}, bf16[640,640]{1,0:T(8,128)(2,1)S(1)}, u32[]{:S(2)}, u32[]{:S(2)}) collective-permute-start(bf16[640,640]{1,0:T(8,128)(2,1)} %collective-permute-done.28), channel_id=1, source_target_pairs={{0,8},{8,0},{16,24},{24,16},{32,40},{40,32},{48,56},{56,48},{64,72... | collective-permute-start | bytes 2457608 | tf_op jit(solution)/shard_map/ppermute | solution.py:37
  165.2 19.6 %collective-permute-start.35 = (bf16[640,640]{1,0:T(8,128)(2,1)}, bf16[640,640]{1,0:T(8,128)(2,1)S(1)}, u32[]{:S(2)}, u32[]{:S(2)}) collective-permute-start(bf16[640,640]{1,0:T(8,128)(2,1)} %collective-permute-done.32), channel_id=1, source_target_pairs={{0,8},{8,0},{16,24},{24,16},{32,40},{40,32},{48,56},{56,48},{64,72... | collective-permute-start | bytes 2457608 | tf_op jit(solution)/shard_map/ppermute | solution.py:37
  165.7 21.5 %collective-permute-start.34 = (bf16[640,640]{1,0:T(8,128)(2,1)}, bf16[640,640]{1,0:T(8,128)(2,1)S(1)}, u32[]{:S(2)}, u32[]{:S(2)}) collective-permute-start(bf16[640,640]{1,0:T(8,128)(2,1)} %collective-permute-done.30), channel_id=1, source_target_pairs={{0,8},{8,0},{16,24},{24,16},{32,40},{40,32},{48,56},{56,48},{64,72... | collective-permute-start | bytes 2457608 | tf_op jit(solution)/shard_map/ppermute | solution.py:37
  165.8 12.8 %collective-permute-start.29 = (bf16[192,640]{1,0:T(8,128)(2,1)S(1)}, bf16[192,640]{1,0:T(8,128)(2,1)S(1)}, u32[]{:S(2)}, u32[]{:S(2)}) collective-permute-start(bf16[192,640]{1,0:T(8,128)(2,1)S(1)} %shard_map.78), channel_id=1, source_target_pairs={{0,2},{1,3},{2,0},{3,1},{4,6},{5,7},{6,4},{7,5},{8,10},{9,11},{10,... | collective-permute-start | bytes 737288 | tf_op jit(solution)/shard_map/ppermute | solution.py:65
  177.1 6.2 %collective-permute-start.31 = (bf16[192,640]{1,0:T(8,128)(2,1)S(1)}, bf16[192,640]{1,0:T(8,128)(2,1)S(1)}, u32[]{:S(2)}, u32[]{:S(2)}) collective-permute-start(bf16[192,640]{1,0:T(8,128)(2,1)S(1)} %shard_map.78), channel_id=1, source_target_pairs={{0,3},{1,0},{2,1},{3,2},{4,7},{5,4},{6,5},{7,6},{8,11},{9,8},{10,9... | collective-permute-start | bytes 737288 | tf_op jit(solution)/shard_map/ppermute | solution.py:65
  187.6 7.8 %collective-permute-start.36 = (bf16[192,640]{1,0:T(8,128)(2,1)S(1)}, bf16[192,640]{1,0:T(8,128)(2,1)S(1)}, u32[]{:S(2)}, u32[]{:S(2)}) collective-permute-start(bf16[192,640]{1,0:T(8,128)(2,1)S(1)} %get-tuple-element.116), channel_id=1, source_target_pairs={{0,4},{1,5},{2,6},{3,7},{4,0},{5,1},{6,2},{7,3},{8,12},{9,13},{10,... | collective-permute-start | bytes 737288 | tf_op jit(solution)/shard_map/ppermute | solution.py:65
